TPU v7x, 32 devices: a whole 2x2x4 slice. The times are simulated.
32 devices in a mesh: facet: 4 (over y, core), base: 8 (over z, x).
Axes of the slice: x: 2, y: 2, z: 4, core: 2. Of those that a mesh axis runs over, the one named last changes fastest.
Arguments:
- facets: bfloat16 [64, 16, 2, 4096], P('base', 'facet'), may hold values from -6 to 6
- observed: bfloat16 [64, 2, 1024], P('base'), may hold values from -6 to 6
- sub_u: int32 [64], P('base'), may hold values from -16384 to 16352
- sub_v: int32 [64], P('base'), may hold values from -16384 to 16352
- sub_block: int32 [64], P('base'), may hold values from 0 to 127
- sub_count: int32 [64], P('base'), may hold values from 0 to 4096, as said below
- gain_real: float32 [128], replicated, may hold values from 0.5 to 1.5
- gain_imag: float32 [128], replicated, may hold values from -0.5 to 0.5
Outputs:
- facet_residual: float32 [64, 16, 2, 4096], P('base', 'facet')
- residual_grids: bfloat16 [64, 2, 1024], P('base')
Inputs may be any that keep to these rules, and one draw needn't show every extreme that they name: `sub_count`: each slot holds a subgrid with that many visibilities, 0 for an empty slot; some slot holds 4096.
All inputs are finite; a program needn't handle non-finite values.
Results may differ from a plain program's by a relative error of at most 0.0053.
Values may be sent and summed in bfloat16 or wider, within the bound.
A program may use at most 256 MiB of HBM per device.

v0:
```python
import math

import jax
import jax.numpy as jnp
from jax import lax
from jax.sharding import PartitionSpec as P

FS = 4096
NPIX = 32768
SG = 32
NF = 16
BLOCKS = 128
CMAX = 4096


def column_tables(facet_id, v_list):
    column_place = (facet_id % 4 + 2) * FS + jnp.arange(FS, dtype=jnp.int32)
    frequency = (v_list[:, None] + jnp.arange(SG, dtype=jnp.int32)[None, :]).reshape(-1)
    cycles = jnp.mod(column_place[:, None] * frequency[None, :], NPIX)
    phases = cycles.astype(jnp.float32) * (2.0 * math.pi / NPIX)
    return (jnp.cos(phases).astype(jnp.bfloat16), jnp.sin(phases).astype(jnp.bfloat16))


def strip_rows(facet_id, row_count, total_rows):
    return (
        (facet_id // 4 + 2) * FS + (FS - total_rows) // 2 + jnp.arange(row_count, dtype=jnp.int32)
    )


def row_tables(u_list, row_place):
    frequency = u_list[:, None] + jnp.arange(SG, dtype=jnp.int32)[None, :]
    cycles = jnp.mod(frequency[:, :, None] * row_place[None, None, :], NPIX)
    phases = cycles.astype(jnp.float32) * (2.0 * math.pi / NPIX)
    return (jnp.cos(phases).astype(jnp.bfloat16), jnp.sin(phases).astype(jnp.bfloat16))


def along_columns(left, table):
    return lax.dot_general(
        left, table, (((1,), (1,)), ((), ())), preferred_element_type=jnp.float32
    )


def batched(form, left, right):
    return jnp.einsum(form, left, right, preferred_element_type=jnp.float32)


def degrid_piece(block_rows, col_cos, col_sin, row_cos, row_sin):
    row_count = block_rows.shape[0]
    slots = row_cos.shape[0]
    real_rows = block_rows[:, 0, :]
    imag_rows = block_rows[:, 1, :]
    strip_real = jnp.dot(real_rows, col_cos, preferred_element_type=jnp.float32) + jnp.dot(
        imag_rows, col_sin, preferred_element_type=jnp.float32
    )
    strip_imag = jnp.dot(imag_rows, col_cos, preferred_element_type=jnp.float32) - jnp.dot(
        real_rows, col_sin, preferred_element_type=jnp.float32
    )
    strip_real = strip_real.astype(jnp.bfloat16).reshape(row_count, slots, SG)
    strip_imag = strip_imag.astype(jnp.bfloat16).reshape(row_count, slots, SG)
    model_real = batched("npk,knq->npq", row_cos, strip_real) + batched(
        "npk,knq->npq", row_sin, strip_imag
    )
    model_imag = batched("npk,knq->npq", row_cos, strip_imag) - batched(
        "npk,knq->npq", row_sin, strip_real
    )
    return jnp.stack([model_real, model_imag], 1).reshape(slots, 2, SG * SG)


def grid_piece(residual_block, col_cos, col_sin, row_cos, row_sin):
    slots = residual_block.shape[0]
    row_count = row_cos.shape[2]
    cells = residual_block.reshape(slots, 2, SG, SG)
    cell_real = cells[:, 0]
    cell_imag = cells[:, 1]
    lift_real = batched("npk,npq->knq", row_cos, cell_real) - batched(
        "npk,npq->knq", row_sin, cell_imag
    )
    lift_imag = batched("npk,npq->knq", row_cos, cell_imag) + batched(
        "npk,npq->knq", row_sin, cell_real
    )
    lift_real = lift_real.reshape(row_count, slots * SG).astype(jnp.bfloat16)
    lift_imag = lift_imag.reshape(row_count, slots * SG).astype(jnp.bfloat16)
    grid_real = along_columns(lift_real, col_cos) - along_columns(lift_imag, col_sin)
    grid_imag = along_columns(lift_real, col_sin) + along_columns(lift_imag, col_cos)
    return jnp.stack([grid_real, grid_imag], 1)


def weighted_residual(model, observed, sub_block, sub_count, gain_real, gain_imag):
    block_hits = sub_block[:, None] == jnp.arange(BLOCKS, dtype=jnp.int32)[None, :]
    gain_re_rows = jnp.sum(jnp.where(block_hits, gain_real[None, :], 0.0), axis=1)[:, None]
    gain_im_rows = jnp.sum(jnp.where(block_hits, gain_imag[None, :], 0.0), axis=1)[:, None]
    weight = (sub_count.astype(jnp.float32) / CMAX)[:, None]
    seen = observed.astype(jnp.float32)
    model_real = model[:, 0]
    model_imag = model[:, 1]
    diff_real = seen[:, 0] - (gain_re_rows * model_real - gain_im_rows * model_imag)
    diff_imag = seen[:, 1] - (gain_re_rows * model_imag + gain_im_rows * model_real)
    out_real = weight * (gain_re_rows * diff_real + gain_im_rows * diff_imag)
    out_imag = weight * (gain_re_rows * diff_imag - gain_im_rows * diff_real)
    return jnp.stack([out_real, out_imag], 1).astype(jnp.bfloat16)


def per_device(facets, observed, sub_u, sub_v, sub_block, sub_count, gain_real, gain_imag):
    local_rows = facets.shape[0]
    local_facets = facets.shape[1]
    local_subgrids = sub_u.shape[0]
    total_rows = local_rows * lax.axis_size("base")
    norm_scale = 1.0 / math.sqrt(NF * total_rows * FS)
    facet_first = lax.axis_index("facet") * local_facets
    facet_ids = [facet_first + position for position in range(local_facets)]
    initial = jnp.zeros((local_subgrids, 2, SG * SG), jnp.float32)
    tables = [column_tables(facet_id, sub_v) for facet_id in facet_ids]
    summed = initial
    block_rows = lax.all_gather(facets, "base", axis=0, tiled=True)
    row_count = block_rows.shape[0]
    for position in range(local_facets):
        row_cos, row_sin = row_tables(sub_u, strip_rows(facet_ids[position], row_count, total_rows))
        summed = summed + degrid_piece(
            block_rows[:, position], tables[position][0], tables[position][1], row_cos, row_sin
        )
    model = lax.psum(summed, "facet") * norm_scale
    residual = weighted_residual(model, observed, sub_block, sub_count, gain_real, gain_imag)
    grid_tables = [column_tables(facet_id, sub_v) for facet_id in facet_ids]
    pieces = []
    for position in range(local_facets):
        row_cos, row_sin = row_tables(
            sub_u, strip_rows(facet_ids[position], local_rows * lax.axis_size("base"), total_rows)
        )
        pieces.append(
            grid_piece(
                residual, grid_tables[position][0], grid_tables[position][1], row_cos, row_sin
            )
        )
    facet_sum = lax.psum_scatter(jnp.stack(pieces, 1), "base", scatter_dimension=0, tiled=True)
    return (facet_sum * norm_scale, residual)


def solution(mesh):
    in_specs = (
        P("base", "facet", None, None),
        P("base", None, None),
        P("base"),
        P("base"),
        P("base"),
        P("base"),
        P(),
        P(),
    )
    out_specs = (P("base", "facet", None, None), P("base", None, None))
    return jax.shard_map(
        per_device, mesh=mesh, in_specs=in_specs, out_specs=out_specs, check_vma=False
    )
```

profile of v0, /device:TPU:0, one launch (start us, length us, event | category | flops | bytes accessed | tf_op | source)
XLA Modules:
  0.0 830.3 jit_solution(13239372118887005453)
XLA Ops:
  11.7 75.1 %all-gather.2.cloned.1.call-done = bf16[64,4,2,4096]{3,0,2,1:T(8,128)(2,1)} async-done(((bf16[8,4,2,4096]{3,0,2,1:T(8,128)(2,1)}), bf16[64,4,2,4096]{3,0,2,1:T(8,128)(2,1)}) %all-gather.2.cloned.1.call-update) | async-done | bytes 4194320 | tf_op jit(solution)/shard_map/all_gather | solution.py:114
  120.8 16.6 %fusion.27 = f32[256,64]{0,1:T(8,128)} fusion(s32[256]{0:T(256)S(1)} %add.454, s32[4096]{0:T(1024)S(1)} %iota_add_fusion.1, bf16[64,2,4096]{2,0,1:T(8,128)(2,1)S(1)} %get-tuple-element.17), kind=kOutput, calls=%fused_computation.68 | convolution fusion | flops 149946368 | bytes 607232 | tf_op jit(solution)/shard_map/dot_general | solution.py:52
  137.4 16.2 %fusion.28 = f32[256,64]{0,1:T(8,128)} fusion(s32[256]{0:T(256)S(1)} %add.454, s32[4096]{0:T(1024)S(1)} %iota_add_fusion.1, bf16[64,2,4096]{2,0,1:T(8,128)(2,1)S(1)} %get-tuple-element.17), kind=kOutput, calls=%fused_computation.69 | convolution fusion | flops 149946368 | bytes 607232 | tf_op jit(solution)/shard_map/dot_general | solution.py:55
  153.6 16.2 %fusion.21 = f32[256,64]{0,1:T(8,128)} fusion(s32[256]{0:T(256)S(1)} %add.454, s32[4096]{0:T(1024)S(1)} %iota_add_fusion.2, bf16[64,2,4096]{2,0,1:T(8,128)(2,1)S(1)} %get-tuple-element.18), kind=kOutput, calls=%fused_computation.62 | convolution fusion | flops 149946368 | bytes 607232 | tf_op jit(solution)/shard_map/dot_general | solution.py:52
  169.8 16.6 %fusion.22 = f32[256,64]{0,1:T(8,128)} fusion(s32[256]{0:T(256)S(1)} %add.454, s32[4096]{0:T(1024)S(1)} %iota_add_fusion.2, bf16[64,2,4096]{2,0,1:T(8,128)(2,1)S(1)} %get-tuple-element.18), kind=kOutput, calls=%fused_computation.63 | convolution fusion | flops 149946368 | bytes 607232 | tf_op jit(solution)/shard_map/dot_general | solution.py:55
  186.4 16.2 %fusion.39 = f32[256,64]{0,1:T(8,128)} fusion(s32[256]{0:T(256)S(1)} %add.454, s32[4096]{0:T(1024)S(1)} %iota_add_fusion.3, bf16[64,2,4096]{2,0,1:T(8,128)(2,1)S(1)} %get-tuple-element.19), kind=kOutput, calls=%fused_computation.80 | convolution fusion | flops 149946368 | bytes 607232 | tf_op jit(solution)/shard_map/dot_general | solution.py:52
  202.6 16.4 %fusion.40 = f32[256,64]{0,1:T(8,128)} fusion(s32[256]{0:T(256)S(1)} %add.454, s32[4096]{0:T(1024)S(1)} %iota_add_fusion.3, bf16[64,2,4096]{2,0,1:T(8,128)(2,1)S(1)} %get-tuple-element.19), kind=kOutput, calls=%fused_computation.81 | convolution fusion | flops 149946368 | bytes 607232 | tf_op jit(solution)/shard_map/dot_general | solution.py:55
  219.0 16.1 %fusion.71 = bf16[64,256]{1,0:T(8,128)(2,1)S(1)} fusion(f32[256,64]{0,1:T(8,128)S(1)} %fusion.33, s32[256]{0:T(256)S(1)} %add.454, s32[4096]{0:T(1024)S(1)} %iota_add_fusion, bf16[64,2,4096]{2,0,1:T(8,128)(2,1)S(1)} %get-tuple-element.16), kind=kOutput, calls=%fused_computation.128 | convolution fusion | flops 149979136 | bytes 640000 | tf_op jit(solution)/shard_map/dot_general | solution.py:52
  235.2 19.6 %fusion.70 = bf16[64,256]{1,0:T(8,128)(2,1)S(1)} fusion(f32[256,64]{0,1:T(8,128)S(1)} %fusion.34, s32[256]{0:T(256)S(1)} %add.454, s32[4096]{0:T(1024)S(1)} %iota_add_fusion, bf16[64,2,4096]{2,0,1:T(8,128)(2,1)} %copy-done), kind=kOutput, calls=%fused_computation.127 | convolution fusion | flops 149979136 | bytes 640000 | tf_op jit(solution)/shard_map/dot_general | solution.py:55
  254.9 16.5 %fusion.73 = bf16[64,256]{1,0:T(8,128)(2,1)S(1)} fusion(f32[256,64]{0,1:T(8,128)} %fusion.27, s32[256]{0:T(256)S(1)} %add.454, s32[4096]{0:T(1024)S(1)} %iota_add_fusion.1, bf16[64,2,4096]{2,0,1:T(8,128)(2,1)S(1)} %get-tuple-element.17), kind=kOutput, calls=%fused_computation.130 | convolution fusion | flops 149979136 | bytes 640000 | tf_op jit(solution)/shard_map/dot_general | solution.py:52
  271.6 16.6 %fusion.72 = bf16[64,256]{1,0:T(8,128)(2,1)S(1)} fusion(f32[256,64]{0,1:T(8,128)} %fusion.28, s32[256]{0:T(256)S(1)} %add.454, s32[4096]{0:T(1024)S(1)} %iota_add_fusion.1, bf16[64,2,4096]{2,0,1:T(8,128)(2,1)S(1)} %get-tuple-element.17), kind=kOutput, calls=%fused_computation.129 | convolution fusion | flops 149979136 | bytes 640000 | tf_op jit(solution)/shard_map/dot_general | solution.py:55
  288.3 17.0 %fusion.75 = bf16[64,256]{1,0:T(8,128)(2,1)S(1)} fusion(f32[256,64]{0,1:T(8,128)} %fusion.21, s32[256]{0:T(256)S(1)} %add.454, s32[4096]{0:T(1024)S(1)} %iota_add_fusion.2, bf16[64,2,4096]{2,0,1:T(8,128)(2,1)S(1)} %get-tuple-element.18), kind=kOutput, calls=%fused_computation.132 | convolution fusion | flops 149979136 | bytes 640000 | tf_op jit(solution)/shard_map/dot_general | solution.py:52
  321.3 15.9 %fusion.69 = bf16[64,256]{1,0:T(8,128)(2,1)S(1)} fusion(f32[256,64]{0,1:T(8,128)S(1)} %copy-done.6, s32[256]{0:T(256)S(1)} %add.454, s32[4096]{0:T(1024)S(1)} %iota_add_fusion.3, bf16[64,2,4096]{2,0,1:T(8,128)(2,1)S(1)} %get-tuple-element.19), kind=kOutput, calls=%fused_computation.126 | convolution fusion | flops 149979136 | bytes 640000 | tf_op jit(solution)/shard_map/dot_general | solution.py:52
  337.3 15.9 %fusion.68 = bf16[64,256]{1,0:T(8,128)(2,1)S(1)} fusion(f32[256,64]{0,1:T(8,128)S(1)} %copy-done.5, s32[256]{0:T(256)S(1)} %add.454, s32[4096]{0:T(1024)S(1)} %iota_add_fusion.3, bf16[64,2,4096]{2,0,1:T(8,128)(2,1)S(1)} %get-tuple-element.19), kind=kOutput, calls=%fused_computation.125 | convolution fusion | flops 149979136 | bytes 640000 | tf_op jit(solution)/shard_map/dot_general | solution.py:55
  366.8 28.8 %all-reduce.2.cloned.1.call-done = f32[8,2,1024]{2,1,0:T(2,128)} async-done(((f32[8,2,1024]{2,1,0:T(2,128)}), f32[8,2,1024]{2,1,0:T(2,128)}) %all-reduce.2.cloned.1.call-update) | async-done | bytes 65552 | tf_op jit(solution)/shard_map/psum | solution.py:121
  403.3 16.0 %fusion.41 = f32[64,4096]{1,0:T(8,128)S(1)} fusion(bf16[64,256]{0,1:T(8,128)(2,1)S(1)} %bitcast.186, s32[256]{0:T(256)S(1)} %add.454, s32[4096]{0:T(1024)S(1)} %iota_add_fusion.3), kind=kOutput, calls=%fused_computation.82 | convolution fusion | flops 149946368 | bytes 1098752 | tf_op jit(solution)/shard_map/dot_general | solution.py:38
  419.3 16.3 %fusion.38 = f32[64,4096]{1,0:T(8,128)S(1)} fusion(bf16[64,256]{0,1:T(8,128)(2,1)S(1)} %bitcast.187, s32[256]{0:T(256)S(1)} %add.454, s32[4096]{0:T(1024)S(1)} %iota_add_fusion.3), kind=kOutput, calls=%fused_computation.79 | convolution fusion | flops 149946368 | bytes 1098752 | tf_op jit(solution)/shard_map/dot_general | solution.py:38
  436.4 16.0 %fusion.23 = f32[64,4096]{1,0:T(8,128)S(1)} fusion(bf16[64,256]{0,1:T(8,128)(2,1)S(1)} %bitcast.188, s32[256]{0:T(256)S(1)} %add.454, s32[4096]{0:T(1024)S(1)} %iota_add_fusion.2), kind=kOutput, calls=%fused_computation.64 | convolution fusion | flops 149946368 | bytes 1098752 | tf_op jit(solution)/shard_map/dot_general | solution.py:38
  452.4 15.9 %fusion.20 = f32[64,4096]{1,0:T(8,128)S(1)} fusion(bf16[64,256]{0,1:T(8,128)(2,1)S(1)} %bitcast.189, s32[256]{0:T(256)S(1)} %add.454, s32[4096]{0:T(1024)S(1)} %iota_add_fusion.2), kind=kOutput, calls=%fused_computation.61 | convolution fusion | flops 149946368 | bytes 1098752 | tf_op jit(solution)/shard_map/dot_general | solution.py:38
  469.5 16.0 %fusion.29 = f32[64,4096]{1,0:T(8,128)S(1)} fusion(bf16[64,256]{0,1:T(8,128)(2,1)S(1)} %bitcast.190, s32[256]{0:T(256)S(1)} %add.454, s32[4096]{0:T(1024)S(1)} %iota_add_fusion.1), kind=kOutput, calls=%fused_computation.70 | convolution fusion | flops 149946368 | bytes 1098752 | tf_op jit(solution)/shard_map/dot_general | solution.py:38
  485.5 15.9 %fusion.26 = f32[64,4096]{1,0:T(8,128)S(1)} fusion(bf16[64,256]{0,1:T(8,128)(2,1)S(1)} %bitcast.191, s32[256]{0:T(256)S(1)} %add.454, s32[4096]{0:T(1024)S(1)} %iota_add_fusion.1), kind=kOutput, calls=%fused_computation.67 | convolution fusion | flops 149946368 | bytes 1098752 | tf_op jit(solution)/shard_map/dot_general | solution.py:38
  502.2 16.4 %fusion.35 = f32[64,4096]{1,0:T(8,128)S(1)} fusion(bf16[64,256]{0,1:T(8,128)(2,1)S(1)} %bitcast.184, s32[256]{0:T(256)S(1)} %add.454, s32[4096]{0:T(1024)S(1)} %iota_add_fusion), kind=kOutput, calls=%fused_computation.76 | convolution fusion | flops 149946368 | bytes 1098752 | tf_op jit(solution)/shard_map/dot_general | solution.py:38
  518.6 15.9 %fusion.32 = f32[64,4096]{1,0:T(8,128)S(1)} fusion(bf16[64,256]{0,1:T(8,128)(2,1)S(1)} %bitcast.185, s32[256]{0:T(256)S(1)} %add.454, s32[4096]{0:T(1024)S(1)} %iota_add_fusion), kind=kOutput, calls=%fused_computation.73 | convolution fusion | flops 149946368 | bytes 1098752 | tf_op jit(solution)/shard_map/dot_general | solution.py:38
  537.3 16.3 %fusion.1 = f32[64,1,4096]{2,0,1:T(8,128)S(1)} fusion(f32[64,4096]{1,0:T(8,128)S(1)} %fusion.41, bf16[64,256]{0,1:T(8,128)(2,1)S(1)} %bitcast.182, s32[256]{0:T(256)S(1)} %add.454, s32[4096]{0:T(1024)S(1)} %iota_add_fusion.3), kind=kOutput, calls=%fused_computation.30 | convolution fusion | flops 150208512 | bytes 2147328 | tf_op jit(solution)/shard_map/dot_general | solution.py:38
  553.7 16.1 %fusion = f32[64,1,4096]{2,0,1:T(8,128)S(1)} fusion(f32[64,4096]{1,0:T(8,128)S(1)} %fusion.38, bf16[64,256]{0,1:T(8,128)(2,1)S(1)} %bitcast.183, s32[256]{0:T(256)S(1)} %add.454, s32[4096]{0:T(1024)S(1)} %iota_add_fusion.3), kind=kOutput, calls=%fused_computation.29 | convolution fusion | flops 150208512 | bytes 2147328 | tf_op jit(solution)/shard_map/dot_general | solution.py:38
  569.8 16.2 %fusion.3 = f32[64,1,4096]{2,0,1:T(8,128)S(1)} fusion(f32[64,4096]{1,0:T(8,128)S(1)} %fusion.23, bf16[64,256]{0,1:T(8,128)(2,1)S(1)} %bitcast.180, s32[256]{0:T(256)S(1)} %add.454, s32[4096]{0:T(1024)S(1)} %iota_add_fusion.2), kind=kOutput, calls=%fused_computation.32 | convolution fusion | flops 150208512 | bytes 2147328 | tf_op jit(solution)/shard_map/dot_general | solution.py:38
  585.9 16.3 %fusion.2 = f32[64,1,4096]{2,0,1:T(8,128)S(1)} fusion(f32[64,4096]{1,0:T(8,128)S(1)} %fusion.20, bf16[64,256]{0,1:T(8,128)(2,1)S(1)} %bitcast.181, s32[256]{0:T(256)S(1)} %add.454, s32[4096]{0:T(1024)S(1)} %iota_add_fusion.2), kind=kOutput, calls=%fused_computation.31 | convolution fusion | flops 150208512 | bytes 2147328 | tf_op jit(solution)/shard_map/dot_general | solution.py:38
  602.2 16.2 %fusion.5 = f32[64,1,4096]{2,0,1:T(8,128)S(1)} fusion(f32[64,4096]{1,0:T(8,128)S(1)} %fusion.29, bf16[64,256]{0,1:T(8,128)(2,1)S(1)} %bitcast.178, s32[256]{0:T(256)S(1)} %add.454, s32[4096]{0:T(1024)S(1)} %iota_add_fusion.1), kind=kOutput, calls=%fused_computation.34 | convolution fusion | flops 150208512 | bytes 2147328 | tf_op jit(solution)/shard_map/dot_general | solution.py:38
  618.4 16.1 %fusion.4 = f32[64,1,4096]{2,0,1:T(8,128)S(1)} fusion(f32[64,4096]{1,0:T(8,128)S(1)} %fusion.26, bf16[64,256]{0,1:T(8,128)(2,1)S(1)} %bitcast.179, s32[256]{0:T(256)S(1)} %add.454, s32[4096]{0:T(1024)S(1)} %iota_add_fusion.1), kind=kOutput, calls=%fused_computation.33 | convolution fusion | flops 150208512 | bytes 2147328 | tf_op jit(solution)/shard_map/dot_general | solution.py:38
  634.5 16.4 %fusion.7 = f32[64,1,4096]{2,0,1:T(8,128)S(1)} fusion(f32[64,4096]{1,0:T(8,128)S(1)} %fusion.35, bf16[64,256]{0,1:T(8,128)(2,1)S(1)} %bitcast.176, s32[256]{0:T(256)S(1)} %add.454, s32[4096]{0:T(1024)S(1)} %iota_add_fusion), kind=kOutput, calls=%fused_computation.36 | convolution fusion | flops 150208512 | bytes 2147328 | tf_op jit(solution)/shard_map/dot_general | solution.py:38
  650.9 16.1 %fusion.6 = f32[64,1,4096]{2,0,1:T(8,128)S(1)} fusion(f32[64,4096]{1,0:T(8,128)S(1)} %fusion.32, bf16[64,256]{0,1:T(8,128)(2,1)S(1)} %bitcast.177, s32[256]{0:T(256)S(1)} %add.454, s32[4096]{0:T(1024)S(1)} %iota_add_fusion), kind=kOutput, calls=%fused_computation.35 | convolution fusion | flops 150208512 | bytes 2147328 | tf_op jit(solution)/shard_map/dot_general | solution.py:38
  672.1 148.4 %reduce-scatter.2.cloned.1.call-done = f32[8,4,2,4096]{3,0,2,1:T(8,128)} async-done(((f32[64,4,2,4096]{3,0,2,1:T(8,128)}), f32[8,4,2,4096]{3,0,2,1:T(8,128)}) %reduce-scatter.2.cloned.1.call-update) | async-done | bytes 1048592 | tf_op jit(solution)/shard_map/reduce_scatter | solution.py:134
  (101 shorter events, 89.5 us)
Async XLA Ops:
  7.2 79.7 %all-gather.2.cloned.1.call-start = ((), (), s32[]{:S(2)}) async-start(), calls=%async_computation.1 | async-start | bytes 4718592 | tf_op jit(solution)/shard_map/all_gather | solution.py:114
  9.4 386.2 %all-reduce.2.cloned.1.call-start = ((), (), s32[]{:S(2)}) async-start(), calls=%async_computation.2 | async-start | bytes 131072 | tf_op jit(solution)/shard_map/psum | solution.py:121
  89.4 129.6 %copy-start = (bf16[64,2,4096]{2,0,1:T(8,128)(2,1)}, bf16[64,2,4096]{2,0,1:T(8,128)(2,1)S(1)}, u32[]{:S(2)}) copy-start(bf16[64,2,4096]{2,0,1:T(8,128)(2,1)S(1)} %get-tuple-element.16) | copy-start | bytes 3145732
  288.3 17.1 %copy-start.7 = (f32[256,64]{0,1:T(8,128)S(1)}, f32[256,64]{0,1:T(8,128)}, u32[]{:S(2)}) copy-start(f32[256,64]{0,1:T(8,128)} %fusion.22) | copy-start | bytes 196612
  305.4 15.9 %copy-start.6 = (f32[256,64]{0,1:T(8,128)S(1)}, f32[256,64]{0,1:T(8,128)}, u32[]{:S(2)}) copy-start(f32[256,64]{0,1:T(8,128)} %fusion.39) | copy-start | bytes 196612
  321.2 16.1 %copy-start.5 = (f32[256,64]{0,1:T(8,128)S(1)}, f32[256,64]{0,1:T(8,128)}, u32[]{:S(2)}) copy-start(f32[256,64]{0,1:T(8,128)} %fusion.40) | copy-start | bytes 196612
  357.0 9.5 %copy-start.2 = (f32[128]{0:T(128)S(1)}, f32[128]{0:T(128)}, u32[]{:S(2)}) copy-start(f32[128]{0:T(128)} %param.14) | copy-start | bytes 1540
  357.0 9.6 %copy-start.3 = (s32[8]{0:T(128)S(1)}, s32[8]{0:T(128)}, u32[]{:S(2)}) copy-start(s32[8]{0:T(128)} %param.12) | copy-start | bytes 100
  357.0 9.6 %copy-start.4 = (f32[128]{0:T(128)S(1)}, f32[128]{0:T(128)}, u32[]{:S(2)}) copy-start(f32[128]{0:T(128)} %param.15) | copy-start | bytes 1540
  357.0 9.8 %copy-start.1 = (bf16[8,2,1024]{2,1,0:T(2,128)(2,1)S(1)}, bf16[8,2,1024]{2,1,0:T(2,128)(2,1)}, u32[]{:S(2)}) copy-start(bf16[8,2,1024]{2,1,0:T(2,128)(2,1)} %param.9) | copy-start | bytes 98308
  366.1 454.5 %reduce-scatter.2.cloned.1.call-start = ((), (), s32[]{:S(2)}) async-start(), calls=%async_computation.3 | async-start | bytes 9437184 | tf_op jit(solution)/shard_map/reduce_scatter | solution.py:134
Sparse Core Ops, SparseCore 0:
  10.8 76.0 all-gather.1
  366.2 29.3 all-reduce.1
  671.5 148.9 reduce-scatter.1
where the time goes:
time: 840 us; the launch traced here: 830 us
  matrix products  543 us (65%)
  waiting for transfers between devices  252 us (30%)
  between operations  14.5 us (2%)
  other arithmetic  11 us (1%)
  local copies, waits for them, and re-layouts  8.65 us (1%)
    dot_general x16, matrix products, along_columns(): lax.dot_general(left, table, (((1,), (1,)), ((), ())), preferred_element_...  258 us
    reduce_scatter x1, waiting for transfers between devices, per_device(): lax.psum_scatter(jnp.stack(pieces, 1), 'base', scatter_dimension=0, tiled...  148 us
    all_gather x1, waiting for transfers between devices, per_device(): block_rows = lax.all_gather(facets, 'base', axis=0, tiled=True)  75.1 us
    dot_general x4, matrix products, degrid_piece(): jnp.dot(real_rows, col_sin, preferred_element_type=jnp.float32)  67.8 us
    dot_general x4, matrix products, degrid_piece(): jnp.dot(imag_rows, col_sin, preferred_element_type=jnp.float32)  65.5 us
    dot_general x4, matrix products, degrid_piece(): jnp.dot(real_rows, col_cos, preferred_element_type=jnp.float32)  64.9 us
    dot_general x4, matrix products, degrid_piece(): jnp.dot(imag_rows, col_cos, preferred_element_type=jnp.float32)  64.7 us
    psum x1, waiting for transfers between devices, per_device(): model = lax.psum(summed, 'facet') * norm_scale  28.8 us
  transfers between devices with their start and end apart: 3, of which 3 were waited for; matrix products, arithmetic and copies ran while one was open for 0% of the time, Pallas kernels for 0%

commit v1 on v0

v1 whole, which is shorter than its diff:
```python
import functools
import math

import jax
import jax.numpy as jnp
from jax import lax
from jax.experimental import pallas as pl
from jax.experimental.pallas import tpu as pltpu
from jax.sharding import PartitionSpec as P

FS = 4096
NPIX = 32768
SG = 32
NF = 16
CMAX = 4096
QUARTER = NPIX // 4
MESH = pl.DeviceIdType.MESH

LOW = 256
HIGH = FS // LOW
COLS = 4
ROWS = 8
SLOTS = 8
LANES = SLOTS * SG
STEP = 16


def cos_turns(turns):
    away = jnp.abs(((turns + NPIX // 2) & (NPIX - 1)) - NPIX // 2)
    x = (QUARTER - away).astype(jnp.float32) * (2.0 * math.pi / NPIX)
    x2 = x * x
    tail = -1.0 / 39916800
    for term in (362880, -5040, 120, -6):
        tail = tail * x2 + 1.0 / term
    return x + x * (x2 * tail)


def iota(shape, dim):
    return lax.broadcasted_iota(jnp.int32, shape, dim)


def per_lane(values, shape):
    owner = iota(shape, len(shape) - 1) // SG
    out = jnp.full(shape, values[0])
    for s in range(1, SLOTS):
        out = jnp.where(owner == s, values[s], out)
    return out


def kernel(
    n, nf, scale,
    v_ref, u_ref, block_ref, count_ref, gain_re_ref, gain_im_ref, seen_ref, facet_ref,
    out_ref, res_ref,
    freq, low_table, high_table, row_table, product, strip_out, strip, model, lift, lifted, spread,
    v_send, v_recv, s_send, s_recv, m_send, m_recv, l_send, l_recv,
):
    me = lax.axis_index("base")
    mf = lax.axis_index("facet")

    def on_base(k):
        return {"base": lax.rem(me + k, n)}

    def on_facet(k):
        return {"facet": lax.rem(mf + k, nf)}

    barrier = pltpu.get_barrier_semaphore()

    def greet_base(k, _):
        pl.semaphore_signal(barrier, inc=1, device_id=on_base(k), device_id_type=MESH)
        return 0

    lax.fori_loop(1, n, greet_base, 0)
    for k in range(1, nf):
        pl.semaphore_signal(barrier, inc=1, device_id=on_facet(k), device_id_type=MESH)

    own_freq = per_lane([v_ref[s] for s in range(SLOTS)], (8, LANES)) + iota((8, LANES), 1) % SG
    freq[me] = own_freq

    pl.semaphore_wait(barrier, n - 1 + nf - 1)

    def v_copy(k, slot):
        return pltpu.make_async_remote_copy(
            src_ref=freq.at[me], dst_ref=freq.at[slot], send_sem=v_send.at[k],
            recv_sem=v_recv.at[k], device_id=on_base(k), device_id_type=MESH,
        )

    def send_v(k, _):
        v_copy(k, me).start()
        return 0

    lax.fori_loop(1, n, send_v, 0)

    wide = n * 2 * ROWS
    lane = iota((2 * SG, wide), 1)
    sub = iota((2 * SG, wide), 0)
    place = (mf + 2) * FS + (FS - n * ROWS) // 2 + lane // (2 * ROWS) * ROWS + lane % ROWS
    turn = (sub // SG - lane // ROWS % 2) * QUARTER
    for s in range(SLOTS):
        row_table[pl.ds(s * 2 * SG, 2 * SG), :] = cos_turns(
            (sub % SG + u_ref[s]) * place + turn
        ).astype(jnp.bfloat16)

    def strip_copy(k, slot):
        return pltpu.make_async_remote_copy(
            src_ref=strip_out.at[k], dst_ref=strip.at[slot], send_sem=s_send.at[k],
            recv_sem=s_recv.at[k], device_id=on_base(k), device_id_type=MESH,
        )

    def degrid(k, _):
        g = lax.rem(me + k, n)

        @pl.when(k > 0)
        def _():
            v_copy(n - k, g).wait_recv()

        f = freq[g]
        line = iota((HIGH, 8, LANES), 1)
        y = (line % COLS + 2) * FS + iota((HIGH, 8, LANES), 0) * LOW
        high_table[g] = cos_turns(f[None] * y - line // COLS * QUARTER)
        fine = iota((STEP, LANES), 0)
        f2 = jnp.concatenate([f, f], 0)
        fine_cos = cos_turns(f2 * fine)
        fine_sin = cos_turns(f2 * fine - QUARTER)
        step_cos = cos_turns(f2 * fine * STEP)
        step_sin = cos_turns(f2 * fine * STEP - QUARTER)
        for i in range(LOW // STEP):
            c = step_cos[i : i + 1]
            s = step_sin[i : i + 1]
            rows = pl.ds(i * STEP, STEP)
            low_table[g, rows, 0:LANES] = (c * fine_cos - s * fine_sin).astype(jnp.bfloat16)
            low_table[g, rows, LANES : 2 * LANES] = (s * fine_cos + c * fine_sin).astype(
                jnp.bfloat16
            )
        product[...] = jnp.dot(
            facet_ref[...], low_table[g], preferred_element_type=jnp.float32
        ).reshape(HIGH, 2 * COLS * ROWS, 2 * LANES)

        def fold(h, total):
            total_re, total_im = total
            table = high_table[g, h]
            for b in range(COLS):
                re = pl.ds(b * ROWS, ROWS)
                im = pl.ds((COLS + b) * ROWS, ROWS)
                part_re = product[h, re, 0:LANES] + product[h, im, LANES : 2 * LANES]
                part_im = product[h, im, 0:LANES] - product[h, re, LANES : 2 * LANES]
                c = table[b : b + 1]
                s = table[COLS + b : COLS + b + 1]
                total_re = total_re + (part_re * c + part_im * s)
                total_im = total_im + (part_im * c - part_re * s)
            return total_re, total_im

        zero = jnp.zeros((ROWS, LANES), jnp.float32)
        total_re, total_im = lax.fori_loop(0, HIGH, fold, (zero, zero))
        chunk = jnp.concatenate([total_re, total_im], 0).astype(jnp.bfloat16)

        @pl.when(k == 0)
        def _():
            strip[me] = chunk

        @pl.when(k > 0)
        def _():
            strip_out[k] = chunk
            strip_copy(k, me).start()

        return 0

    lax.fori_loop(0, n, degrid, 0)

    def take_strip(k, _):
        strip_copy(k, lax.rem(me + n - k, n)).wait_recv()
        return 0

    lax.fori_loop(1, n, take_strip, 0)

    owner = iota((2 * SG, LANES), 1) // SG
    crossed = jnp.dot(
        row_table[...], strip[...].reshape(wide, LANES), preferred_element_type=jnp.float32
    )
    part = jnp.zeros((2 * SG, LANES), jnp.float32)
    for s in range(SLOTS):
        part = jnp.where(owner == s, crossed[s * 2 * SG : (s + 1) * 2 * SG], part)
    model[mf] = part

    def model_copy(k, slot):
        return pltpu.make_async_remote_copy(
            src_ref=model.at[mf], dst_ref=model.at[slot], send_sem=m_send.at[k],
            recv_sem=m_recv.at[k], device_id=on_facet(k), device_id_type=MESH,
        )

    for k in range(1, nf):
        model_copy(k, mf).start()

    half = (SG, LANES)
    gain_re = per_lane([gain_re_ref[block_ref[s]] for s in range(SLOTS)], half)
    gain_im = per_lane([gain_im_ref[block_ref[s]] for s in range(SLOTS)], half)
    weight = per_lane([count_ref[s] for s in range(SLOTS)], half).astype(jnp.float32) / CMAX
    seen = seen_ref[...].astype(jnp.float32)

    for k in range(1, nf):
        model_copy(k, lax.rem(mf + nf - k, nf)).wait_recv()

    whole = model[0]
    for other in range(1, nf):
        whole = whole + model[other]
    whole = whole * scale
    model_re = whole[:SG]
    model_im = whole[SG:]
    diff_re = seen[:SG] - (gain_re * model_re - gain_im * model_im)
    diff_im = seen[SG:] - (gain_re * model_im + gain_im * model_re)
    res_re = weight * (gain_re * diff_re + gain_im * diff_im)
    res_im = weight * (gain_re * diff_im - gain_im * diff_re)
    residual = jnp.concatenate([res_re, res_im], 0)
    res_ref[...] = residual.astype(jnp.bfloat16)

    blocks = jnp.concatenate(
        [jnp.where(owner == s, residual, 0.0).astype(jnp.bfloat16) for s in range(SLOTS)], 0
    )
    raised = lax.dot_general(
        row_table[...], blocks, (((0,), (0,)), ((), ())), preferred_element_type=jnp.float32
    )
    lift[...] = raised.astype(jnp.bfloat16).reshape(n, 2 * ROWS, LANES)

    def lift_copy(k, slot):
        return pltpu.make_async_remote_copy(
            src_ref=lift.at[lax.rem(me + k, n)], dst_ref=lifted.at[slot], send_sem=l_send.at[k],
            recv_sem=l_recv.at[k], device_id=on_base(k), device_id_type=MESH,
        )

    def send_lift(k, _):
        lift_copy(k, me).start()
        return 0

    lax.fori_loop(1, n, send_lift, 0)
    lifted[me] = lift[me]

    def grid(k, _):
        g = lax.rem(me + n - k, n)

        @pl.when(k > 0)
        def _():
            lift_copy(k, g).wait_recv()

        value = lifted[g].astype(jnp.float32) * scale
        value_re = value[:ROWS]
        value_im = value[ROWS:]

        def turn_one(h, _):
            table = high_table[g, h]
            re = []
            im = []
            for b in range(COLS):
                c = table[b : b + 1]
                s = table[COLS + b : COLS + b + 1]
                re.append(value_re * c - value_im * s)
                im.append(value_re * s + value_im * c)
            re = jnp.concatenate(re, 0)
            im = jnp.concatenate(im, 0)
            half_rows = COLS * ROWS
            spread[h, 0:half_rows, 0:LANES] = re.astype(jnp.bfloat16)
            spread[h, 0:half_rows, LANES : 2 * LANES] = (-im).astype(jnp.bfloat16)
            spread[h, half_rows : 2 * half_rows, 0:LANES] = im.astype(jnp.bfloat16)
            spread[h, half_rows : 2 * half_rows, LANES : 2 * LANES] = re.astype(jnp.bfloat16)
            return 0

        lax.fori_loop(0, HIGH, turn_one, 0)
        term = lax.dot_general(
            spread[...].reshape(HIGH * 2 * COLS * ROWS, 2 * LANES),
            low_table[g],
            (((1,), (1,)), ((), ())),
            preferred_element_type=jnp.float32,
        )

        @pl.when(k == 0)
        def _():
            out_ref[...] = term

        @pl.when(k > 0)
        def _():
            out_ref[...] += term

        return 0

    lax.fori_loop(0, n, grid, 0)

    def drain(k, _):
        v_copy(k, me).wait_send()
        strip_copy(k, me).wait_send()
        lift_copy(k, me).wait_send()
        return 0

    lax.fori_loop(1, n, drain, 0)
    for k in range(1, nf):
        model_copy(k, mf).wait_send()


def per_device(facets, observed, sub_u, sub_v, sub_block, sub_count, gain_real, gain_imag):
    n = lax.axis_size("base")
    nf = lax.axis_size("facet")
    assert facets.shape == (ROWS, COLS, 2, FS) and nf * COLS == NF
    assert observed.shape == (SLOTS, 2, SG * SG)
    scale = 1.0 / math.sqrt(NF * n * ROWS * FS)
    rows = facets.reshape(ROWS, COLS, 2, HIGH, LOW).transpose(3, 2, 1, 0, 4).reshape(-1, LOW)
    seen = observed.reshape(SLOTS, 2, SG, SG).transpose(1, 2, 0, 3).reshape(2 * SG, LANES)
    smem = pl.BlockSpec(memory_space=pltpu.SMEM)
    vmem = pl.BlockSpec(memory_space=pltpu.VMEM)
    bf16 = jnp.bfloat16
    f32 = jnp.float32
    dma = pltpu.SemaphoreType.DMA
    out, res = pl.pallas_call(
        functools.partial(kernel, n, nf, scale),
        out_shape=(
            jax.ShapeDtypeStruct((HIGH * 2 * COLS * ROWS, LOW), f32),
            jax.ShapeDtypeStruct((2 * SG, LANES), bf16),
        ),
        in_specs=[smem] * 6 + [vmem] * 2,
        out_specs=(vmem, vmem),
        scratch_shapes=[
            pltpu.VMEM((n, 8, LANES), jnp.int32),
            pltpu.VMEM((n, LOW, 2 * LANES), bf16),
            pltpu.VMEM((n, HIGH, 8, LANES), f32),
            pltpu.VMEM((SLOTS * 2 * SG, n * 2 * ROWS), bf16),
            pltpu.VMEM((HIGH, 2 * COLS * ROWS, 2 * LANES), f32),
            pltpu.VMEM((n, 2 * ROWS, LANES), bf16),
            pltpu.VMEM((n, 2 * ROWS, LANES), bf16),
            pltpu.VMEM((nf, 2 * SG, LANES), f32),
            pltpu.VMEM((n, 2 * ROWS, LANES), bf16),
            pltpu.VMEM((n, 2 * ROWS, LANES), bf16),
            pltpu.VMEM((HIGH, 2 * COLS * ROWS, 2 * LANES), bf16),
            dma((n,)), dma((n,)), dma((n,)), dma((n,)),
            dma((nf,)), dma((nf,)), dma((n,)), dma((n,)),
        ],
        compiler_params=pltpu.CompilerParams(
            collective_id=0, has_side_effects=True, vmem_limit_bytes=48 * 1024 * 1024
        ),
    )(sub_v, sub_u, sub_block, sub_count, gain_real, gain_imag, seen, rows)
    out = out.reshape(HIGH, 2, COLS, ROWS, LOW).transpose(3, 2, 1, 0, 4)
    res = res.reshape(2, SG, SLOTS, SG).transpose(2, 0, 1, 3)
    return (out.reshape(ROWS, COLS, 2, FS), res.reshape(SLOTS, 2, SG * SG))


def solution(mesh):
    in_specs = (
        P("base", "facet", None, None),
        P("base", None, None),
        P("base"),
        P("base"),
        P("base"),
        P("base"),
        P(),
        P(),
    )
    out_specs = (P("base", "facet", None, None), P("base", None, None))
    return jax.shard_map(
        per_device, mesh=mesh, in_specs=in_specs, out_specs=out_specs, check_vma=False
    )
```

time: 840 us -> 40.8 us (0.05); the launches traced: 830 us -> 40.6 us
  matrix products: 543 us -> 0 us
  waiting for transfers between devices: 252 us -> 0 us
  Pallas kernels: 0 us -> 34.2 us
  between operations: 14.5 us -> 0.75 us
  other arithmetic: 11 us -> 0 us
    dot_general x64 -> x0, matrix products: 543 us -> none  [the longest x16 258 us: along_columns(): lax.dot_general(left, table, (((1,), (1,)), ((), ())), preferred_element_...]
    reduce_scatter x1 -> x0, waiting for transfers between devices: 148 us -> none  [per_device(): lax.psum_scatter(jnp.stack(pieces, 1), 'base', scatter_dimension=0, tiled...]
    all_gather x1 -> x0, waiting for transfers between devices: 75.1 us -> none  [per_device(): block_rows = lax.all_gather(facets, 'base', axis=0, tiled=True)]
    pallas_call x0 -> x1, Pallas kernels: none -> 34.2 us  [per_device(): pl.pallas_call(functools.partial(kernel, n, nf, scale), out_shape=(jax.Sh...]
    psum x1 -> x0, waiting for transfers between devices: 28.8 us -> none  [per_device(): model = lax.psum(summed, 'facet') * norm_scale]
  transfers between devices with their start and end apart: 3 -> 0, of which waited for: 3 -> 0; matrix products, arithmetic and copies ran while one was open for 0% -> 0% of each run, Pallas kernels for 0% -> 0%
where the time goes in v1:
time: 40.8 us; the launch traced here: 40.6 us
  Pallas kernels  34.2 us (84%)
  local copies, waits for them, and re-layouts  5.68 us (14%)
  between operations  0.75 us (2%)
    pallas_call x1, Pallas kernels, per_device(): pl.pallas_call(functools.partial(kernel, n, nf, scale), out_shape=(jax.Sh...  34.2 us
    reshape x2, local copies, waits for them, and re-layouts, per_device(): return (out.reshape(ROWS, COLS, 2, FS), res.reshape(SLOTS, 2, SG * SG))  2.44 us
    reshape x3, local copies, waits for them, and re-layouts, per_device(): observed.reshape(SLOTS, 2, SG, SG).transpose(1, 2, 0, 3)  1.17 us

profile of v1, /device:TPU:0, one launch (start us, length us, event | category | flops | bytes accessed | tf_op | source)
XLA Modules:
  0.0 40.6 jit_solution(2687181112618741215)
XLA Ops:
  0.6 0.0 copy-start.6
  0.6 1.0 %reshape.28 = bf16[8,2,32,32]{3,2,1,0:T(8,128)(2,1)S(1)} reshape(bf16[8,2,1024]{2,1,0:T(2,128)(2,1)} %param.9) | data formatting | bytes 65536 | tf_op jit(solution)/shard_map/reshape | solution.py:303
  1.6 0.1 copy.15
  1.7 0.1 reshape.29.seen_ref
  1.8 0.0 copy-done.6
  1.8 0.3 reshape.30
  2.2 0.0 copy-start.3
  2.2 0.0 copy-start.4
  2.2 0.0 copy-start.5
  2.2 0.3 copy.11
  2.5 0.0 copy-start
  2.5 0.0 copy-start.1
  2.5 0.0 copy-start.2
  2.6 0.3 copy-done.3
  2.8 0.0 copy-done.4
  2.9 0.0 copy-done.5
  2.9 0.3 copy-done
  3.2 0.0 copy-done.1
  3.2 0.0 copy-done.2
  3.2 34.2 %shard_map.95 = (f32[1024,256]{1,0:T(8,128)S(1)}, bf16[64,256]{1,0:T(8,128)(2,1)S(1)}) custom-call(s32[8]{0:T(128)S(1)} %copy-done, s32[8]{0:T(128)S(1)} %copy-done.1, s32[8]{0:T(128)S(1)} %copy-done.2, s32[8]{0:T(128)S(1)} %copy-done.3, f32[128]{0:T(128)S(1)} %copy-done.4, f32[128]{0:T(128)S(1)} %copy-done.5, bf16[64,256]{1,0:T(8,128)(2,1)S(1)} %reshape.29.seen_ref, ...), custom_call_target="tpu_custom_call" | custom-call | tf_op jit(solution)/shard_map/pallas_call | solution.py:309
  37.4 0.6 %copy.12 = f32[8,4,2,16,256]{4,3,2,1,0:T(8,128)S(1)} copy(f32[8,4,2,16,256]{4,0,1,2,3:T(8,128)S(1)} %bitcast.17) | data formatting | bytes 2097152 | tf_op jit(solution)/shard_map/transpose | solution.py:336
  38.0 1.7 %reshape.33 = f32[8,4,2,4096]{3,2,1,0:T(2,128)} reshape(f32[8,4,2,16,256]{4,3,2,1,0:T(8,128)S(1)} %copy.12) | data formatting | bytes 2097152 | tf_op jit(solution)/shard_map/reshape | solution.py:338
  39.7 0.1 reshape.34
  39.8 0.8 %reshape.35 = bf16[8,2,1024]{2,1,0:T(2,128)(2,1)} reshape(bf16[8,2,32,32]{3,2,1,0:T(8,128)(2,1)S(1)} %copy.13) | data formatting | bytes 65536 | tf_op jit(solution)/shard_map/reshape | solution.py:338
  (1 shorter events, 0.0 us)
Async XLA Ops:
  0.6 1.2 %copy-start.6 = (bf16[8,4,2,4096]{3,2,1,0:T(2,128)(2,1)S(1)}, bf16[8,4,2,4096]{3,2,1,0:T(2,128)(2,1)}, u32[]{:S(2)}) copy-start(bf16[8,4,2,4096]{3,2,1,0:T(2,128)(2,1)} %param.8) | copy-start | bytes 1572868
  2.2 0.7 %copy-start.3 = (s32[8]{0:T(128)S(1)}, s32[8]{0:T(128)}, u32[]{:S(2)}) copy-start(s32[8]{0:T(128)} %count_ref.1) | copy-start | bytes 100
  2.2 0.7 %copy-start.4 = (f32[128]{0:T(128)S(1)}, f32[128]{0:T(128)}, u32[]{:S(2)}) copy-start(f32[128]{0:T(128)} %gain_re_ref.1) | copy-start | bytes 1540
  2.2 0.7 %copy-start.5 = (f32[128]{0:T(128)S(1)}, f32[128]{0:T(128)}, u32[]{:S(2)}) copy-start(f32[128]{0:T(128)} %gain_im_ref.1) | copy-start | bytes 1540
  2.5 0.7 %copy-start = (s32[8]{0:T(128)S(1)}, s32[8]{0:T(128)}, u32[]{:S(2)}) copy-start(s32[8]{0:T(128)} %v_ref.1) | copy-start | bytes 100
  2.5 0.7 %copy-start.1 = (s32[8]{0:T(128)S(1)}, s32[8]{0:T(128)}, u32[]{:S(2)}) copy-start(s32[8]{0:T(128)} %u_ref.1) | copy-start | bytes 100
  2.5 0.7 %copy-start.2 = (s32[8]{0:T(128)S(1)}, s32[8]{0:T(128)}, u32[]{:S(2)}) copy-start(s32[8]{0:T(128)} %block_ref.1) | copy-start | bytes 100

commit v2 on v1

v2 whole, which is shorter than its diff:
```python
import functools
import math

import jax
import jax.numpy as jnp
from jax import lax
from jax.experimental import pallas as pl
from jax.experimental.pallas import tpu as pltpu
from jax.sharding import PartitionSpec as P

FS = 4096
NPIX = 32768
SG = 32
NF = 16
CMAX = 4096
QUARTER = NPIX // 4
MESH = pl.DeviceIdType.MESH

LOW = 512
HIGH = FS // LOW
COLS = 4
ROWS = 8
SLOTS = 8
LANES = SLOTS * SG
STEP = 16


def cos_turns(turns):
    away = jnp.abs(((turns + NPIX // 2) & (NPIX - 1)) - NPIX // 2)
    x = (QUARTER - away).astype(jnp.float32) * (2.0 * math.pi / NPIX)
    x2 = x * x
    tail = -1.0 / 39916800
    for term in (362880, -5040, 120, -6):
        tail = tail * x2 + 1.0 / term
    return x + x * (x2 * tail)


def iota(shape, dim):
    return lax.broadcasted_iota(jnp.int32, shape, dim)


def per_lane(values, shape):
    owner = iota(shape, len(shape) - 1) // SG
    out = jnp.full(shape, values[0])
    for s in range(1, SLOTS):
        out = jnp.where(owner == s, values[s], out)
    return out


def kernel(
    n, nf, scale,
    v_ref, u_ref, block_ref, count_ref, gain_re_ref, gain_im_ref, seen_ref, facet_ref,
    out_ref, res_ref,
    freq, low_table, high_one, high_two, row_table, product, strip_out, strip, lift, lifted, spread,
    v_send, v_recv, s_send, s_recv, l_send, l_recv,
):
    me = lax.axis_index("base")
    mf = lax.axis_index("facet")

    def device(k, j):
        return {"base": lax.rem(me + k, n), "facet": lax.rem(mf + j, nf)}

    barrier = pltpu.get_barrier_semaphore()

    def greet(k, _):
        for j in range(nf):
            pl.semaphore_signal(barrier, inc=1, device_id=device(k, j), device_id_type=MESH)
        return 0

    lax.fori_loop(1, n, greet, 0)
    for j in range(1, nf):
        pl.semaphore_signal(barrier, inc=1, device_id=device(0, j), device_id_type=MESH)

    freq[me] = per_lane([v_ref[s] for s in range(SLOTS)], (8, LANES)) + iota((8, LANES), 1) % SG

    wide = n * 2 * ROWS
    lane = iota((2 * SG, wide), 1)
    sub = iota((2 * SG, wide), 0)
    turn = (sub // SG - lane // ROWS % 2) * QUARTER
    first = (FS - n * ROWS) // 2 + lane // (2 * ROWS) * ROWS + lane % ROWS

    def fill_rows(s, _):
        u = sub % SG + u_ref[s]
        for a in range(nf):
            row_table[a, pl.ds(pl.multiple_of(s * 2 * SG, 2 * SG), 2 * SG), :] = cos_turns(
                u * (first + (a + 2) * FS) + turn
            ).astype(jnp.bfloat16)
        return 0

    lax.fori_loop(0, SLOTS, fill_rows, 0)

    pl.semaphore_wait(barrier, n * nf - 1)

    def v_copy(k, slot):
        return pltpu.make_async_remote_copy(
            src_ref=freq.at[me], dst_ref=freq.at[slot], send_sem=v_send.at[k],
            recv_sem=v_recv.at[k], device_id=device(k, 0), device_id_type=MESH,
        )

    def send_v(k, _):
        v_copy(k, me).start()
        return 0

    lax.fori_loop(1, n, send_v, 0)

    def strip_copy(k, j, from_facet, from_base):
        return pltpu.make_async_remote_copy(
            src_ref=strip_out.at[k], dst_ref=strip.at[from_facet, from_base],
            send_sem=s_send.at[k, j], recv_sem=s_recv.at[k, j],
            device_id=device(k, j), device_id_type=MESH,
        )

    def degrid(k, _):
        g = lax.rem(me + k, n)

        @pl.when(k > 0)
        def _():
            v_copy(n - k, g).wait_recv()

        f = freq[g]
        line = iota((8, LANES), 0)
        for h in range(HIGH):
            high = f * ((line // 2 + 2) * FS + h * LOW) - line % 2 * QUARTER
            high_one[g, h] = cos_turns(high)
            high_two[g, h] = cos_turns(high + QUARTER)
        fine = iota((STEP, LANES), 0)
        f2 = jnp.concatenate([f, f], 0)
        fine_cos = cos_turns(f2 * fine)
        fine_sin = cos_turns(f2 * fine - QUARTER)
        for i in range(LOW // STEP):
            if i % STEP == 0:
                steps = f2 * ((fine + i) * STEP)
                step_cos = cos_turns(steps)
                step_sin = cos_turns(steps - QUARTER)
            c = step_cos[i % STEP : i % STEP + 1]
            s = step_sin[i % STEP : i % STEP + 1]
            rows = pl.ds(i * STEP, STEP)
            low_table[g, rows, 0:LANES] = (c * fine_cos - s * fine_sin).astype(jnp.bfloat16)
            low_table[g, rows, LANES : 2 * LANES] = (s * fine_cos + c * fine_sin).astype(
                jnp.bfloat16
            )
        tall = jnp.concatenate([facet_ref[:, h * LOW : (h + 1) * LOW] for h in range(HIGH)], 0)
        product[...] = jnp.dot(tall, low_table[g], preferred_element_type=jnp.float32)
        lines_re = []
        lines_im = []
        for r in range(ROWS):
            total_re = jnp.zeros((8, LANES), jnp.float32)
            total_im = jnp.zeros((8, LANES), jnp.float32)
            for h in range(HIGH):
                rows = pl.ds((h * ROWS + r) * 8, 8)
                part_cos = product[rows, 0:LANES]
                part_sin = product[rows, LANES : 2 * LANES]
                one = high_one[g, h]
                two = high_two[g, h]
                total_re = total_re + (part_cos * one + part_sin * two)
                total_im = total_im + (part_cos * two - part_sin * one)
            lines_re.append(jnp.sum(total_re, 0, keepdims=True))
            lines_im.append(jnp.sum(total_im, 0, keepdims=True))
        chunk = jnp.concatenate(lines_re + lines_im, 0).astype(jnp.bfloat16)
        strip_out[k] = chunk

        @pl.when(k == 0)
        def _():
            strip[mf, me] = chunk

        @pl.when(k > 0)
        def _():
            strip_copy(k, 0, mf, me).start()

        for j in range(1, nf):
            strip_copy(k, j, mf, me).start()
        return 0

    lax.fori_loop(0, n, degrid, 0)

    half = (SG, LANES)
    gain_re = per_lane([gain_re_ref[block_ref[s]] for s in range(SLOTS)], half)
    gain_im = per_lane([gain_im_ref[block_ref[s]] for s in range(SLOTS)], half)
    weight = per_lane([count_ref[s] for s in range(SLOTS)], half).astype(jnp.float32) / CMAX
    seen = seen_ref[...].astype(jnp.float32)

    def take_strip(k, j):
        strip_copy(k, j, lax.rem(mf + nf - j, nf), lax.rem(me + n - k, n)).wait_recv()

    def take_strips(k, _):
        for j in range(nf):
            take_strip(k, j)
        return 0

    for j in range(1, nf):
        take_strip(0, j)
    lax.fori_loop(1, n, take_strips, 0)

    owner = iota((2 * SG, LANES), 1) // SG
    crossed = jnp.zeros((SLOTS * 2 * SG, LANES), jnp.float32)
    for a in range(nf):
        crossed = crossed + jnp.dot(
            row_table[a], strip[a].reshape(wide, LANES), preferred_element_type=jnp.float32
        )
    whole = jnp.zeros((2 * SG, LANES), jnp.float32)
    for s in range(SLOTS):
        whole = jnp.where(owner == s, crossed[s * 2 * SG : (s + 1) * 2 * SG], whole)
    whole = whole * scale
    model_re = whole[:SG]
    model_im = whole[SG:]
    diff_re = seen[:SG] - (gain_re * model_re - gain_im * model_im)
    diff_im = seen[SG:] - (gain_re * model_im + gain_im * model_re)
    res_re = weight * (gain_re * diff_re + gain_im * diff_im)
    res_im = weight * (gain_re * diff_im - gain_im * diff_re)
    residual = jnp.concatenate([res_re, res_im], 0)
    res_ref[...] = residual.astype(jnp.bfloat16)

    blocks = jnp.concatenate(
        [jnp.where(owner == s, residual, 0.0).astype(jnp.bfloat16) for s in range(SLOTS)], 0
    )
    raised = lax.dot_general(
        row_table[mf], blocks, (((0,), (0,)), ((), ())), preferred_element_type=jnp.float32
    )
    lift[...] = raised.astype(jnp.bfloat16).reshape(n, 2 * ROWS, LANES)

    def lift_copy(k, slot):
        return pltpu.make_async_remote_copy(
            src_ref=lift.at[lax.rem(me + k, n)], dst_ref=lifted.at[slot], send_sem=l_send.at[k],
            recv_sem=l_recv.at[k], device_id=device(k, 0), device_id_type=MESH,
        )

    def send_lift(k, _):
        lift_copy(k, me).start()
        return 0

    lax.fori_loop(1, n, send_lift, 0)
    lifted[me] = lift[me]

    def grid(k, _):
        g = lax.rem(me + n - k, n)

        @pl.when(k > 0)
        def _():
            lift_copy(k, g).wait_recv()

        value = lifted[g].astype(jnp.float32) * scale
        for h in range(HIGH):
            one = high_one[g, h]
            two = high_two[g, h]
            for r in range(0, ROWS, 2):
                by_cos = []
                by_sin = []
                for t in (r, r + 1):
                    re = value[t : t + 1]
                    im = value[ROWS + t : ROWS + t + 1]
                    by_cos.append(re * one + im * two)
                    by_sin.append(re * two - im * one)
                rows = pl.ds((h * ROWS + r) * 8, 16)
                spread[rows, 0:LANES] = jnp.concatenate(by_cos, 0).astype(jnp.bfloat16)
                spread[rows, LANES : 2 * LANES] = jnp.concatenate(by_sin, 0).astype(jnp.bfloat16)
        term = lax.dot_general(
            spread[...], low_table[g], (((1,), (1,)), ((), ())), preferred_element_type=jnp.float32
        )

        def lay(add):
            for h in range(HIGH):
                part = term[h * 8 * ROWS : (h + 1) * 8 * ROWS]
                at = pl.ds(h * LOW, LOW)
                out_ref[:, at] = out_ref[:, at] + part if add else part

        @pl.when(k == 0)
        def _():
            lay(False)

        @pl.when(k > 0)
        def _():
            lay(True)

        return 0

    lax.fori_loop(0, n, grid, 0)

    def drain(k, _):
        v_copy(k, me).wait_send()
        lift_copy(k, me).wait_send()
        for j in range(nf):
            strip_copy(k, j, mf, me).wait_send()
        return 0

    lax.fori_loop(1, n, drain, 0)
    for j in range(1, nf):
        strip_copy(0, j, mf, me).wait_send()


def per_device(facets, observed, sub_u, sub_v, sub_block, sub_count, gain_real, gain_imag):
    n = lax.axis_size("base")
    nf = lax.axis_size("facet")
    assert facets.shape == (ROWS, COLS, 2, FS) and nf * COLS == NF
    assert observed.shape == (SLOTS, 2, SG * SG)
    scale = 1.0 / math.sqrt(NF * n * ROWS * FS)
    rows = facets.reshape(ROWS * COLS * 2, FS)
    seen = observed.reshape(SLOTS, 2, SG, SG).transpose(1, 2, 0, 3).reshape(2 * SG, LANES)
    smem = pl.BlockSpec(memory_space=pltpu.SMEM)
    vmem = pl.BlockSpec(memory_space=pltpu.VMEM)
    bf16 = jnp.bfloat16
    f32 = jnp.float32
    dma = pltpu.SemaphoreType.DMA
    out, res = pl.pallas_call(
        functools.partial(kernel, n, nf, scale),
        out_shape=(
            jax.ShapeDtypeStruct((ROWS * COLS * 2, FS), f32),
            jax.ShapeDtypeStruct((2 * SG, LANES), bf16),
        ),
        in_specs=[smem] * 6 + [vmem] * 2,
        out_specs=(vmem, vmem),
        scratch_shapes=[
            pltpu.VMEM((n, 8, LANES), jnp.int32),
            pltpu.VMEM((n, LOW, 2 * LANES), bf16),
            pltpu.VMEM((n, HIGH, 8, LANES), f32),
            pltpu.VMEM((n, HIGH, 8, LANES), f32),
            pltpu.VMEM((nf, SLOTS * 2 * SG, n * 2 * ROWS), bf16),
            pltpu.VMEM((HIGH * ROWS * 8, 2 * LANES), f32),
            pltpu.VMEM((n, 2 * ROWS, LANES), bf16),
            pltpu.VMEM((nf, n, 2 * ROWS, LANES), bf16),
            pltpu.VMEM((n, 2 * ROWS, LANES), bf16),
            pltpu.VMEM((n, 2 * ROWS, LANES), bf16),
            pltpu.VMEM((HIGH * ROWS * 8, 2 * LANES), bf16),
            dma((n,)), dma((n,)), dma((n, nf)), dma((n, nf)), dma((n,)), dma((n,)),
        ],
        compiler_params=pltpu.CompilerParams(
            collective_id=0, has_side_effects=True, vmem_limit_bytes=48 * 1024 * 1024
        ),
    )(sub_v, sub_u, sub_block, sub_count, gain_real, gain_imag, seen, rows)
    res = res.reshape(2, SG, SLOTS, SG).transpose(2, 0, 1, 3)
    return (out.reshape(ROWS, COLS, 2, FS), res.reshape(SLOTS, 2, SG * SG))


def solution(mesh):
    in_specs = (
        P("base", "facet", None, None),
        P("base", None, None),
        P("base"),
        P("base"),
        P("base"),
        P("base"),
        P(),
        P(),
    )
    out_specs = (P("base", "facet", None, None), P("base", None, None))
    return jax.shard_map(
        per_device, mesh=mesh, in_specs=in_specs, out_specs=out_specs, check_vma=False
    )
```

time: 40.8 us -> 34.2 us (0.84)
  Pallas kernels: 34.2 us -> 28.9 us
  local copies, waits for them, and re-layouts: 5.68 us -> 4.37 us
    pallas_call x1, Pallas kernels: 34.2 us -> 28.9 us  [per_device(): pl.pallas_call(functools.partial(kernel, n, nf, scale), out_shape=(jax.Sh...]
    transpose x1 -> x0, local copies, waits for them, and re-layouts: 0.61 us -> none  [per_device(): out = out.reshape(HIGH, 2, COLS, ROWS, LOW).transpose(3, 2, 1, 0, 4)]
    reshape x2 -> x1, local copies, waits for them, and re-layouts: 0.63 us -> 0.2 us  [per_device(): rows = facets.reshape(ROWS * COLS * 2, FS)]
where the time goes in v2:
time: 34.2 us; the launch traced here: 34 us
  Pallas kernels  28.9 us (85%)
  local copies, waits for them, and re-layouts  4.37 us (13%)
  between operations  0.74 us (2%)
    pallas_call x1, Pallas kernels, per_device(): pl.pallas_call(functools.partial(kernel, n, nf, scale), out_shape=(jax.Sh...  28.9 us
    reshape x2, local copies, waits for them, and re-layouts, per_device(): return (out.reshape(ROWS, COLS, 2, FS), res.reshape(SLOTS, 2, SG * SG))  2.37 us
    reshape x3, local copies, waits for them, and re-layouts, per_device(): observed.reshape(SLOTS, 2, SG, SG).transpose(1, 2, 0, 3)  1.17 us

profile of v2, /device:TPU:0, one launch (start us, length us, event | category | flops | bytes accessed | tf_op | source)
XLA Modules:
  0.0 34.0 jit_solution(14442852385665834372)
XLA Ops:
  0.6 0.0 copy-start.6
  0.6 1.0 %reshape.22 = bf16[8,2,32,32]{3,2,1,0:T(8,128)(2,1)S(1)} reshape(bf16[8,2,1024]{2,1,0:T(2,128)(2,1)} %param.9) | data formatting | bytes 65536 | tf_op jit(solution)/shard_map/reshape | solution.py:297
  1.6 0.1 copy.13
  1.7 0.1 reshape.23.seen_ref
  1.8 0.0 copy-done.6
  1.8 0.0 copy-start
  1.8 0.0 copy-start.1
  1.9 0.0 copy-start.2
  1.9 0.0 copy-start.3
  1.9 0.0 copy-start.4
  1.9 0.0 copy-start.5
  1.9 0.2 reshape.24.facet_ref
  2.1 0.4 %copy-done = s32[8]{0:T(128)S(1)} copy-done((s32[8]{0:T(128)S(1)}, s32[8]{0:T(128)}, u32[]{:S(2)}) %copy-start) | copy-done | bytes 56
  2.5 0.0 copy-done.1
  2.5 0.0 copy-done.2
  2.5 0.0 copy-done.3
  2.5 0.0 copy-done.4
  2.6 0.0 copy-done.5
  2.6 28.9 %shard_map.95 = (f32[64,4096]{1,0:T(8,128)S(1)}, bf16[64,256]{1,0:T(8,128)(2,1)S(1)}) custom-call(s32[8]{0:T(128)S(1)} %copy-done, s32[8]{0:T(128)S(1)} %copy-done.1, s32[8]{0:T(128)S(1)} %copy-done.2, s32[8]{0:T(128)S(1)} %copy-done.3, f32[128]{0:T(128)S(1)} %copy-done.4, f32[128]{0:T(128)S(1)} %copy-done.5, bf16[64,256]{1,0:T(8,128)(2,1)S(1)} %reshape.23.seen_ref, ...), custom_call_target="tpu_custom_call" | custom-call | tf_op jit(solution)/shard_map/pallas_call | solution.py:303
  31.5 1.6 %reshape.25 = f32[8,4,2,4096]{3,2,1,0:T(2,128)} reshape(f32[64,4096]{1,0:T(8,128)S(1)} %get-tuple-element.4) | data formatting | bytes 2097152 | tf_op jit(solution)/shard_map/reshape | solution.py:330
  33.1 0.1 reshape.26
  33.2 0.8 %reshape.27 = bf16[8,2,1024]{2,1,0:T(2,128)(2,1)} reshape(bf16[8,2,32,32]{3,2,1,0:T(8,128)(2,1)S(1)} %copy.11) | data formatting | bytes 65536 | tf_op jit(solution)/shard_map/reshape | solution.py:330
  (1 shorter events, 0.0 us)
Async XLA Ops:
  0.6 1.2 %copy-start.6 = (bf16[8,4,2,4096]{3,2,1,0:T(2,128)(2,1)S(1)}, bf16[8,4,2,4096]{3,2,1,0:T(2,128)(2,1)}, u32[]{:S(2)}) copy-start(bf16[8,4,2,4096]{3,2,1,0:T(2,128)(2,1)} %param.8) | copy-start | bytes 1572868
  1.8 0.7 %copy-start = (s32[8]{0:T(128)S(1)}, s32[8]{0:T(128)}, u32[]{:S(2)}) copy-start(s32[8]{0:T(128)} %v_ref.1) | copy-start | bytes 100
  1.8 0.7 %copy-start.1 = (s32[8]{0:T(128)S(1)}, s32[8]{0:T(128)}, u32[]{:S(2)}) copy-start(s32[8]{0:T(128)} %u_ref.1) | copy-start | bytes 100
  1.9 0.7 %copy-start.2 = (s32[8]{0:T(128)S(1)}, s32[8]{0:T(128)}, u32[]{:S(2)}) copy-start(s32[8]{0:T(128)} %block_ref.1) | copy-start | bytes 100
  1.9 0.7 %copy-start.3 = (s32[8]{0:T(128)S(1)}, s32[8]{0:T(128)}, u32[]{:S(2)}) copy-start(s32[8]{0:T(128)} %count_ref.1) | copy-start | bytes 100
  1.9 0.7 %copy-start.4 = (f32[128]{0:T(128)S(1)}, f32[128]{0:T(128)}, u32[]{:S(2)}) copy-start(f32[128]{0:T(128)} %gain_re_ref.1) | copy-start | bytes 1540
  1.9 0.7 %copy-start.5 = (f32[128]{0:T(128)S(1)}, f32[128]{0:T(128)}, u32[]{:S(2)}) copy-start(f32[128]{0:T(128)} %gain_im_ref.1) | copy-start | bytes 1540

commit v3 on v2

--- a/solution.py
+++ b/solution.py
@@ -47,15 +47,63 @@
     return out
 
 
+def turned(one, two, c, s):
+    return one * c + two * s, two * c - one * s
+
+
+def phase_plan():
+    shape = (64, LANES)
+    group = iota(shape, 0) // 8
+    line = iota(shape, 0) % 8
+    facet = (line // 2 + 2) * FS
+    shift = jnp.where(line == 0, 8, 64 << line)
+    distance = jnp.where(group < 2, line, jnp.where(group < 4, line * STEP, facet))
+    distance = jnp.where(group < 6, distance, shift)
+    sine = (group == 1) | (group == 3) | (group == 7)
+    quarter = jnp.where(group == 4, -(line % 2), jnp.where(group == 5, 1 - line % 2, 0))
+    return distance, jnp.where(sine, -1, quarter) * QUARTER
+
+
+def fill_tables(f, distance, quarter, low, one, two):
+    table = cos_turns(jnp.concatenate([f] * 8, 0) * distance[...] + quarter[...])
+
+    def by(i):
+        return table[48 + i : 49 + i], table[56 + i : 57 + i]
+
+    def add(pair, turn):
+        return pair[0] * turn[0] - pair[1] * turn[1], pair[1] * turn[0] + pair[0] * turn[1]
+
+    fine = (table[0:8], table[8:16])
+    more = add(fine, by(0))
+    fine = tuple(jnp.concatenate([x, y], 0) for x, y in zip(fine, more))
+    steps = [(table[16:24], table[24:32])]
+    steps.append(add(steps[0], by(1)))
+    steps += [add(step, by(2)) for step in steps[:2]]
+    lines = [(table[32:40], table[40:48])]
+    for i in range(3):
+        lines += [turned(*line, *by(3 + i)) for line in lines]
+    for h in range(HIGH):
+        one[h] = lines[h][0]
+        two[h] = lines[h][1]
+    for i in range(LOW // STEP):
+        step = tuple(x[i % 8 : i % 8 + 1] for x in steps[i // 8])
+        cos, sin = add(fine, step)
+        rows = pl.ds(i * STEP, STEP)
+        low[rows, 0:LANES] = cos.astype(jnp.bfloat16)
+        low[rows, LANES : 2 * LANES] = sin.astype(jnp.bfloat16)
+
+
 def kernel(
     n, nf, scale,
     v_ref, u_ref, block_ref, count_ref, gain_re_ref, gain_im_ref, seen_ref, facet_ref,
     out_ref, res_ref,
-    freq, low_table, high_one, high_two, row_table, product, strip_out, strip, lift, lifted, spread,
+    freq, distance, quarter, low_even, low_odd, one_even, one_odd, two_even, two_odd, row_table,
+    seen_cells, product_even, product_odd, strip_out, strip, lift, lifted, spread_even, spread_odd,
     v_send, v_recv, s_send, s_recv, l_send, l_recv,
 ):
     me = lax.axis_index("base")
     mf = lax.axis_index("facet")
+    pairs = n // 2
 
     def device(k, j):
         return {"base": lax.rem(me + k, n), "facet": lax.rem(mf + j, nf)}
@@ -72,6 +120,15 @@
         pl.semaphore_signal(barrier, inc=1, device_id=device(0, j), device_id_type=MESH)
 
     freq[me] = per_lane([v_ref[s] for s in range(SLOTS)], (8, LANES)) + iota((8, LANES), 1) % SG
+    distance[...], quarter[...] = phase_plan()
+
+    def even(i):
+        return low_even.at[i], one_even.at[i], two_even.at[i]
+
+    def odd(i):
+        return low_odd.at[i], one_odd.at[i], two_odd.at[i]
+
+    fill_tables(freq[me], distance, quarter, *even(0))
 
     wide = n * 2 * ROWS
     lane = iota((2 * SG, wide), 1)
@@ -89,6 +146,20 @@
 
     lax.fori_loop(0, SLOTS, fill_rows, 0)
 
+    owner = iota((2 * SG, LANES), 1) // SG
+    cells = SG * SG
+    same = iota((SG, cells), 1) // SG == iota((SG, cells), 0)
+    seen = seen_ref[...].astype(jnp.float32)
+    tall = jnp.concatenate(
+        [jnp.where(same, seen[i : i + 1], 0.0).astype(jnp.bfloat16) for i in range(2 * SLOTS)], 0
+    )
+    pick = (iota((cells, LANES), 0) % SG == iota((cells, LANES), 1) % SG).astype(jnp.float32)
+    picked = jnp.dot(tall, pick.astype(jnp.bfloat16), preferred_element_type=jnp.float32)
+    placed = jnp.zeros((2 * SG, LANES), jnp.float32)
+    for s in range(SLOTS):
+        placed = jnp.where(owner == s, picked[s * 2 * SG : (s + 1) * 2 * SG], placed)
+    seen_cells[...] = placed
+
     pl.semaphore_wait(barrier, n * nf - 1)
 
     def v_copy(k, slot):
@@ -110,37 +181,11 @@
             device_id=device(k, j), device_id_type=MESH,
         )
 
-    def degrid(k, _):
-        g = lax.rem(me + k, n)
-
-        @pl.when(k > 0)
-        def _():
-            v_copy(n - k, g).wait_recv()
-
-        f = freq[g]
-        line = iota((8, LANES), 0)
-        for h in range(HIGH):
-            high = f * ((line // 2 + 2) * FS + h * LOW) - line % 2 * QUARTER
-            high_one[g, h] = cos_turns(high)
-            high_two[g, h] = cos_turns(high + QUARTER)
-        fine = iota((STEP, LANES), 0)
-        f2 = jnp.concatenate([f, f], 0)
-        fine_cos = cos_turns(f2 * fine)
-        fine_sin = cos_turns(f2 * fine - QUARTER)
-        for i in range(LOW // STEP):
-            if i % STEP == 0:
-                steps = f2 * ((fine + i) * STEP)
-                step_cos = cos_turns(steps)
-                step_sin = cos_turns(steps - QUARTER)
-            c = step_cos[i % STEP : i % STEP + 1]
-            s = step_sin[i % STEP : i % STEP + 1]
-            rows = pl.ds(i * STEP, STEP)
-            low_table[g, rows, 0:LANES] = (c * fine_cos - s * fine_sin).astype(jnp.bfloat16)
-            low_table[g, rows, LANES : 2 * LANES] = (s * fine_cos + c * fine_sin).astype(
-                jnp.bfloat16
-            )
+    def multiply(low, product):
         tall = jnp.concatenate([facet_ref[:, h * LOW : (h + 1) * LOW] for h in range(HIGH)], 0)
-        product[...] = jnp.dot(tall, low_table[g], preferred_element_type=jnp.float32)
+        product[...] = jnp.dot(tall, low[...], preferred_element_type=jnp.float32)
+
+    def fold(k, product, one, two):
         lines_re = []
         lines_im = []
         for r in range(ROWS):
@@ -150,18 +195,16 @@
                 rows = pl.ds((h * ROWS + r) * 8, 8)
                 part_cos = product[rows, 0:LANES]
                 part_sin = product[rows, LANES : 2 * LANES]
-                one = high_one[g, h]
-                two = high_two[g, h]
-                total_re = total_re + (part_cos * one + part_sin * two)
-                total_im = total_im + (part_cos * two - part_sin * one)
+                total_re = total_re + (part_cos * one[h] + part_sin * two[h])
+                total_im = total_im + (part_cos * two[h] - part_sin * one[h])
             lines_re.append(jnp.sum(total_re, 0, keepdims=True))
             lines_im.append(jnp.sum(total_im, 0, keepdims=True))
-        chunk = jnp.concatenate(lines_re + lines_im, 0).astype(jnp.bfloat16)
-        strip_out[k] = chunk
-
+        strip_out[k] = jnp.concatenate(lines_re + lines_im, 0).astype(jnp.bfloat16)
+
+    def send_strip(k):
         @pl.when(k == 0)
         def _():
-            strip[mf, me] = chunk
+            strip[mf, me] = strip_out[k]
 
         @pl.when(k > 0)
         def _():
@@ -169,15 +212,33 @@
 
         for j in range(1, nf):
             strip_copy(k, j, mf, me).start()
-        return 0
-
-    lax.fori_loop(0, n, degrid, 0)
+
+    def take_v(k):
+        v_copy(n - k, lax.rem(me + k, n)).wait_recv()
+
+    def degrid(i, _):
+        k = 2 * i
+        take_v(k + 1)
+        pl.when(k + 2 < n)(lambda: take_v(k + 2))
+        low, one, two = even(i)
+        multiply(low, product_even)
+        fill_tables(freq[lax.rem(me + k + 1, n)], distance, quarter, *odd(i))
+        fold(k, product_even, one, two)
+        low, one, two = odd(i)
+        multiply(low, product_odd)
+        send_strip(k)
+        fill_tables(freq[lax.rem(me + k + 2, n)], distance, quarter, *even(i + 1))
+        fold(k + 1, product_odd, one, two)
+        send_strip(k + 1)
+        return 0
+
+    lax.fori_loop(0, pairs, degrid, 0)
 
     half = (SG, LANES)
     gain_re = per_lane([gain_re_ref[block_ref[s]] for s in range(SLOTS)], half)
     gain_im = per_lane([gain_im_ref[block_ref[s]] for s in range(SLOTS)], half)
     weight = per_lane([count_ref[s] for s in range(SLOTS)], half).astype(jnp.float32) / CMAX
-    seen = seen_ref[...].astype(jnp.float32)
+    seen = seen_cells[...]
 
     def take_strip(k, j):
         strip_copy(k, j, lax.rem(mf + nf - j, nf), lax.rem(me + n - k, n)).wait_recv()
@@ -191,7 +252,6 @@
         take_strip(0, j)
     lax.fori_loop(1, n, take_strips, 0)
 
-    owner = iota((2 * SG, LANES), 1) // SG
     crossed = jnp.zeros((SLOTS * 2 * SG, LANES), jnp.float32)
     for a in range(nf):
         crossed = crossed + jnp.dot(
@@ -208,7 +268,6 @@
     res_re = weight * (gain_re * diff_re + gain_im * diff_im)
     res_im = weight * (gain_re * diff_im - gain_im * diff_re)
     residual = jnp.concatenate([res_re, res_im], 0)
-    res_ref[...] = residual.astype(jnp.bfloat16)
 
     blocks = jnp.concatenate(
         [jnp.where(owner == s, residual, 0.0).astype(jnp.bfloat16) for s in range(SLOTS)], 0
@@ -231,49 +290,55 @@
     lax.fori_loop(1, n, send_lift, 0)
     lifted[me] = lift[me]
 
-    def grid(k, _):
-        g = lax.rem(me + n - k, n)
-
-        @pl.when(k > 0)
-        def _():
-            lift_copy(k, g).wait_recv()
-
-        value = lifted[g].astype(jnp.float32) * scale
+    grow = (iota((LANES, cells), 0) % SG == iota((LANES, cells), 1) % SG).astype(jnp.float32)
+    grown = jnp.dot(blocks, grow.astype(jnp.bfloat16), preferred_element_type=jnp.float32)
+    lines = [
+        jnp.sum(jnp.where(same, grown[i * SG : (i + 1) * SG], 0.0), 0, keepdims=True)
+        for i in range(2 * SLOTS)
+    ]
+    res_ref[...] = jnp.concatenate(lines, 0).astype(jnp.bfloat16)
+
+    def turn_chunk(k, one, two, spread):
+        value = lifted[lax.rem(me + n - k, n)].astype(jnp.float32) * scale
         for h in range(HIGH):
-            one = high_one[g, h]
-            two = high_two[g, h]
             for r in range(0, ROWS, 2):
                 by_cos = []
                 by_sin = []
                 for t in (r, r + 1):
                     re = value[t : t + 1]
                     im = value[ROWS + t : ROWS + t + 1]
-                    by_cos.append(re * one + im * two)
-                    by_sin.append(re * two - im * one)
+                    by_cos.append(re * one[h] + im * two[h])
+                    by_sin.append(re * two[h] - im * one[h])
                 rows = pl.ds((h * ROWS + r) * 8, 16)
                 spread[rows, 0:LANES] = jnp.concatenate(by_cos, 0).astype(jnp.bfloat16)
                 spread[rows, LANES : 2 * LANES] = jnp.concatenate(by_sin, 0).astype(jnp.bfloat16)
+
+    def gather(spread, low):
         term = lax.dot_general(
-            spread[...], low_table[g], (((1,), (1,)), ((), ())), preferred_element_type=jnp.float32
+            spread[...], low[...], (((1,), (1,)), ((), ())), preferred_element_type=jnp.float32
         )
-
-        def lay(add):
-            for h in range(HIGH):
-                part = term[h * 8 * ROWS : (h + 1) * 8 * ROWS]
-                at = pl.ds(h * LOW, LOW)
-                out_ref[:, at] = out_ref[:, at] + part if add else part
-
-        @pl.when(k == 0)
-        def _():
-            lay(False)
-
-        @pl.when(k > 0)
-        def _():
-            lay(True)
-
-        return 0
-
-    lax.fori_loop(0, n, grid, 0)
+        for h in range(HIGH):
+            out_ref[:, pl.ds(h * LOW, LOW)] += term[h * 8 * ROWS : (h + 1) * 8 * ROWS]
+
+    def take_lift(k):
+        lift_copy(k, lax.rem(me + n - k, n)).wait_recv()
+
+    def grid(i, _):
+        k = 2 * i
+        take_lift(k + 1)
+        low, one, two = odd(pairs - i - 1)
+        gather(spread_even, low_even.at[pairs - i])
+        turn_chunk(k + 1, one, two, spread_odd)
+        pl.when(k + 2 < n)(lambda: take_lift(k + 2))
+        gather(spread_odd, low)
+        _, one, two = even(pairs - i - 1)
+        turn_chunk(lax.rem(k + 2, n), one, two, spread_even)
+        return 0
+
+    out_ref[...] = jnp.zeros(out_ref.shape, jnp.float32)
+    _, one, two = even(pairs)
+    turn_chunk(0, one, two, spread_even)
+    lax.fori_loop(0, pairs, grid, 0)
 
     def drain(k, _):
         v_copy(k, me).wait_send()
@@ -290,11 +355,11 @@
 def per_device(facets, observed, sub_u, sub_v, sub_block, sub_count, gain_real, gain_imag):
     n = lax.axis_size("base")
     nf = lax.axis_size("facet")
-    assert facets.shape == (ROWS, COLS, 2, FS) and nf * COLS == NF
+    assert facets.shape == (ROWS, COLS, 2, FS) and nf * COLS == NF and n % 2 == 0
     assert observed.shape == (SLOTS, 2, SG * SG)
     scale = 1.0 / math.sqrt(NF * n * ROWS * FS)
     rows = facets.reshape(ROWS * COLS * 2, FS)
-    seen = observed.reshape(SLOTS, 2, SG, SG).transpose(1, 2, 0, 3).reshape(2 * SG, LANES)
+    seen = observed.reshape(SLOTS * 2, SG * SG)
     smem = pl.BlockSpec(memory_space=pltpu.SMEM)
     vmem = pl.BlockSpec(memory_space=pltpu.VMEM)
     bf16 = jnp.bfloat16
@@ -304,21 +369,29 @@
         functools.partial(kernel, n, nf, scale),
         out_shape=(
             jax.ShapeDtypeStruct((ROWS * COLS * 2, FS), f32),
-            jax.ShapeDtypeStruct((2 * SG, LANES), bf16),
+            jax.ShapeDtypeStruct((SLOTS * 2, SG * SG), bf16),
         ),
         in_specs=[smem] * 6 + [vmem] * 2,
         out_specs=(vmem, vmem),
         scratch_shapes=[
             pltpu.VMEM((n, 8, LANES), jnp.int32),
-            pltpu.VMEM((n, LOW, 2 * LANES), bf16),
-            pltpu.VMEM((n, HIGH, 8, LANES), f32),
-            pltpu.VMEM((n, HIGH, 8, LANES), f32),
+            pltpu.VMEM((64, LANES), jnp.int32),
+            pltpu.VMEM((64, LANES), jnp.int32),
+            pltpu.VMEM((n // 2 + 1, LOW, 2 * LANES), bf16),
+            pltpu.VMEM((n // 2, LOW, 2 * LANES), bf16),
+            pltpu.VMEM((n // 2 + 1, HIGH, 8, LANES), f32),
+            pltpu.VMEM((n // 2, HIGH, 8, LANES), f32),
+            pltpu.VMEM((n // 2 + 1, HIGH, 8, LANES), f32),
+            pltpu.VMEM((n // 2, HIGH, 8, LANES), f32),
             pltpu.VMEM((nf, SLOTS * 2 * SG, n * 2 * ROWS), bf16),
+            pltpu.VMEM((2 * SG, LANES), f32),
+            pltpu.VMEM((HIGH * ROWS * 8, 2 * LANES), f32),
             pltpu.VMEM((HIGH * ROWS * 8, 2 * LANES), f32),
             pltpu.VMEM((n, 2 * ROWS, LANES), bf16),
             pltpu.VMEM((nf, n, 2 * ROWS, LANES), bf16),
             pltpu.VMEM((n, 2 * ROWS, LANES), bf16),
             pltpu.VMEM((n, 2 * ROWS, LANES), bf16),
+            pltpu.VMEM((HIGH * ROWS * 8, 2 * LANES), bf16),
             pltpu.VMEM((HIGH * ROWS * 8, 2 * LANES), bf16),
             dma((n,)), dma((n,)), dma((n, nf)), dma((n, nf)), dma((n,)), dma((n,)),
         ],
@@ -326,7 +399,6 @@
             collective_id=0, has_side_effects=True, vmem_limit_bytes=48 * 1024 * 1024
         ),
     )(sub_v, sub_u, sub_block, sub_count, gain_real, gain_imag, seen, rows)
-    res = res.reshape(2, SG, SLOTS, SG).transpose(2, 0, 1, 3)
     return (out.reshape(ROWS, COLS, 2, FS), res.reshape(SLOTS, 2, SG * SG))
 
 

time: 34.2 us -> 35 us (1.023)
  Pallas kernels: 28.9 us -> 29.8 us
    reshape x1, local copies, waits for them, and re-layouts: 0.2 us -> 1.26 us  [per_device(): rows = facets.reshape(ROWS * COLS * 2, FS)]
    pallas_call x1, Pallas kernels: 28.9 us -> 29.8 us  [per_device(): pl.pallas_call(functools.partial(kernel, n, nf, scale), out_shape=(jax.Sh...]
    reshape x4 -> x1, local copies, waits for them, and re-layouts: 1.3 us -> 0.78 us  [per_device(): seen = observed.reshape(SLOTS * 2, SG * SG)]
    unnamed x14 -> x12, local copies, waits for them, and re-layouts: 0.49 us -> 0.04 us
where the time goes in v3:
time: 35 us; the launch traced here: 34.8 us
  Pallas kernels  29.8 us (85%)
  local copies, waits for them, and re-layouts  4.3 us (12%)
  between operations  0.74 us (2%)
    pallas_call x1, Pallas kernels, per_device(): pl.pallas_call(functools.partial(kernel, n, nf, scale), out_shape=(jax.Sh...  29.8 us
    reshape x2, local copies, waits for them, and re-layouts, per_device(): return (out.reshape(ROWS, COLS, 2, FS), res.reshape(SLOTS, 2, SG * SG))  2.22 us
    reshape x1, local copies, waits for them, and re-layouts, per_device(): rows = facets.reshape(ROWS * COLS * 2, FS)  1.26 us
    reshape x1, local copies, waits for them, and re-layouts, per_device(): seen = observed.reshape(SLOTS * 2, SG * SG)  0.78 us

profile of v3, /device:TPU:0, one launch (start us, length us, event | category | flops | bytes accessed | tf_op | source)
XLA Modules:
  0.0 34.8 jit_solution(15020854207418147799)
XLA Ops:
  0.6 0.8 %reshape.16.seen_ref = bf16[16,1024]{1,0:T(8,128)(2,1)S(1)} reshape(bf16[8,2,1024]{2,1,0:T(2,128)(2,1)} %param.9) | data formatting | bytes 65536 | tf_op jit(solution)/shard_map/reshape | solution.py:362
  1.4 0.0 copy-start
  1.4 0.0 copy-start.1
  1.4 0.0 copy-start.2
  1.4 0.0 copy-start.3
  1.5 0.0 copy-start.4
  1.5 0.0 copy-start.5
  1.5 1.3 %reshape.17.facet_ref = bf16[64,4096]{1,0:T(8,128)(2,1)S(1)} reshape(bf16[8,4,2,4096]{3,2,1,0:T(2,128)(2,1)} %param.8) | data formatting | bytes 1048576 | tf_op jit(solution)/shard_map/reshape | solution.py:361
  2.7 0.0 copy-done
  2.8 0.0 copy-done.1
  2.8 0.0 copy-done.2
  2.8 0.0 copy-done.3
  2.8 0.0 copy-done.4
  2.8 0.0 copy-done.5
  2.8 29.8 %shard_map.95 = (f32[64,4096]{1,0:T(8,128)S(1)}, bf16[16,1024]{1,0:T(8,128)(2,1)S(1)}) custom-call(s32[8]{0:T(128)S(1)} %copy-done, s32[8]{0:T(128)S(1)} %copy-done.1, s32[8]{0:T(128)S(1)} %copy-done.2, s32[8]{0:T(128)S(1)} %copy-done.3, f32[128]{0:T(128)S(1)} %copy-done.4, f32[128]{0:T(128)S(1)} %copy-done.5, bf16[16,1024]{1,0:T(8,128)(2,1)S(1)} %reshape.16.seen_ref, ...), custom_call_target="tpu_custom_call" | custom-call | tf_op jit(solution)/shard_map/pallas_call | solution.py:368
  32.6 1.6 %reshape.18 = f32[8,4,2,4096]{3,2,1,0:T(2,128)} reshape(f32[64,4096]{1,0:T(8,128)S(1)} %get-tuple-element.4) | data formatting | bytes 2097152 | tf_op jit(solution)/shard_map/reshape | solution.py:402
  34.2 0.6 %reshape.19 = bf16[8,2,1024]{2,1,0:T(2,128)(2,1)} reshape(bf16[16,1024]{1,0:T(8,128)(2,1)S(1)} %get-tuple-element.5) | data formatting | bytes 65536 | tf_op jit(solution)/shard_map/reshape | solution.py:402
Async XLA Ops:
  1.4 1.3 %copy-start = (s32[8]{0:T(128)S(1)}, s32[8]{0:T(128)}, u32[]{:S(2)}) copy-start(s32[8]{0:T(128)} %v_ref.1) | copy-start | bytes 100
  1.4 1.3 %copy-start.1 = (s32[8]{0:T(128)S(1)}, s32[8]{0:T(128)}, u32[]{:S(2)}) copy-start(s32[8]{0:T(128)} %u_ref.1) | copy-start | bytes 100
  1.4 1.3 %copy-start.2 = (s32[8]{0:T(128)S(1)}, s32[8]{0:T(128)}, u32[]{:S(2)}) copy-start(s32[8]{0:T(128)} %block_ref.1) | copy-start | bytes 100
  1.4 1.3 %copy-start.3 = (s32[8]{0:T(128)S(1)}, s32[8]{0:T(128)}, u32[]{:S(2)}) copy-start(s32[8]{0:T(128)} %count_ref.1) | copy-start | bytes 100
  1.5 1.3 %copy-start.4 = (f32[128]{0:T(128)S(1)}, f32[128]{0:T(128)}, u32[]{:S(2)}) copy-start(f32[128]{0:T(128)} %gain_re_ref.1) | copy-start | bytes 1540
  1.5 1.3 %copy-start.5 = (f32[128]{0:T(128)S(1)}, f32[128]{0:T(128)}, u32[]{:S(2)}) copy-start(f32[128]{0:T(128)} %gain_im_ref.1) | copy-start | bytes 1540

commit v4 on v3

--- a/solution.py
+++ b/solution.py
@@ -95,11 +95,12 @@
 
 def kernel(
     n, nf, scale,
-    v_ref, u_ref, block_ref, count_ref, gain_re_ref, gain_im_ref, seen_ref, facet_ref,
+    v_raw, u_raw, block_raw, count_raw, gain_re_raw, gain_im_raw, seen_raw, facet_raw,
     out_ref, res_ref,
-    freq, distance, quarter, low_even, low_odd, one_even, one_odd, two_even, two_odd, row_table,
+    v_ref, u_ref, block_ref, count_ref, gain_re_ref, gain_im_ref, seen_ref, facet_four,
+    facet_ref, freq, distance, quarter, low_even, low_odd, one_even, one_odd, two_even, two_odd, row_table,
     seen_cells, product_even, product_odd, strip_out, strip, lift, lifted, spread_even, spread_odd,
-    v_send, v_recv, s_send, s_recv, l_send, l_recv,
+    v_send, v_recv, s_send, s_recv, l_send, l_recv, in_sem,
 ):
     me = lax.axis_index("base")
     mf = lax.axis_index("facet")
@@ -108,6 +109,14 @@
     def device(k, j):
         return {"base": lax.rem(me + k, n), "facet": lax.rem(mf + j, nf)}
 
+    raw = [v_raw, facet_raw, seen_raw, u_raw, block_raw, count_raw, gain_re_raw, gain_im_raw]
+    held = [v_ref, facet_four, seen_ref, u_ref, block_ref, count_ref, gain_re_ref, gain_im_ref]
+    loads = [
+        pltpu.make_async_copy(src, dst, in_sem.at[i]) for i, (src, dst) in enumerate(zip(raw, held))
+    ]
+    for load in loads:
+        load.start()
+
     barrier = pltpu.get_barrier_semaphore()
 
     def greet(k, _):
@@ -119,6 +128,7 @@
     for j in range(1, nf):
         pl.semaphore_signal(barrier, inc=1, device_id=device(0, j), device_id_type=MESH)
 
+    loads[0].wait()
     freq[me] = per_lane([v_ref[s] for s in range(SLOTS)], (8, LANES)) + iota((8, LANES), 1) % SG
     distance[...], quarter[...] = phase_plan()
 
@@ -128,7 +138,32 @@
     def odd(i):
         return low_odd.at[i], one_odd.at[i], two_odd.at[i]
 
+
+    loads[1].wait()
+    for r in range(0, ROWS, 2):
+        both = []
+        for t in (r, r + 1):
+            both += [facet_four[t, b].astype(jnp.float32) for b in range(COLS)]
+        facet_ref[pl.ds(r * 8, 16), :] = jnp.concatenate(both, 0).astype(jnp.bfloat16)
+
+    pl.semaphore_wait(barrier, n * nf - 1)
+
+    def v_copy(k, slot):
+        return pltpu.make_async_remote_copy(
+            src_ref=freq.at[me], dst_ref=freq.at[slot], send_sem=v_send.at[k],
+            recv_sem=v_recv.at[k], device_id=device(k, 0), device_id_type=MESH,
+        )
+
+    def send_v(k, _):
+        v_copy(k, me).start()
+        return 0
+
+    lax.fori_loop(1, n, send_v, 0)
+
     fill_tables(freq[me], distance, quarter, *even(0))
+
+    for load in loads[2:]:
+        load.wait()
 
     wide = n * 2 * ROWS
     lane = iota((2 * SG, wide), 1)
@@ -149,30 +184,17 @@
     owner = iota((2 * SG, LANES), 1) // SG
     cells = SG * SG
     same = iota((SG, cells), 1) // SG == iota((SG, cells), 0)
-    seen = seen_ref[...].astype(jnp.float32)
-    tall = jnp.concatenate(
-        [jnp.where(same, seen[i : i + 1], 0.0).astype(jnp.bfloat16) for i in range(2 * SLOTS)], 0
-    )
+    tall = []
+    for s in range(SLOTS):
+        seen = seen_ref[s].astype(jnp.float32)
+        tall += [jnp.where(same, seen[i : i + 1], 0.0).astype(jnp.bfloat16) for i in range(2)]
+    tall = jnp.concatenate(tall, 0)
     pick = (iota((cells, LANES), 0) % SG == iota((cells, LANES), 1) % SG).astype(jnp.float32)
     picked = jnp.dot(tall, pick.astype(jnp.bfloat16), preferred_element_type=jnp.float32)
     placed = jnp.zeros((2 * SG, LANES), jnp.float32)
     for s in range(SLOTS):
         placed = jnp.where(owner == s, picked[s * 2 * SG : (s + 1) * 2 * SG], placed)
     seen_cells[...] = placed
-
-    pl.semaphore_wait(barrier, n * nf - 1)
-
-    def v_copy(k, slot):
-        return pltpu.make_async_remote_copy(
-            src_ref=freq.at[me], dst_ref=freq.at[slot], send_sem=v_send.at[k],
-            recv_sem=v_recv.at[k], device_id=device(k, 0), device_id_type=MESH,
-        )
-
-    def send_v(k, _):
-        v_copy(k, me).start()
-        return 0
-
-    lax.fori_loop(1, n, send_v, 0)
 
     def strip_copy(k, j, from_facet, from_base):
         return pltpu.make_async_remote_copy(
@@ -218,10 +240,10 @@
 
     def degrid(i, _):
         k = 2 * i
+        low, one, two = even(i)
+        multiply(low, product_even)
         take_v(k + 1)
         pl.when(k + 2 < n)(lambda: take_v(k + 2))
-        low, one, two = even(i)
-        multiply(low, product_even)
         fill_tables(freq[lax.rem(me + k + 1, n)], distance, quarter, *odd(i))
         fold(k, product_even, one, two)
         low, one, two = odd(i)
@@ -358,9 +380,7 @@
     assert facets.shape == (ROWS, COLS, 2, FS) and nf * COLS == NF and n % 2 == 0
     assert observed.shape == (SLOTS, 2, SG * SG)
     scale = 1.0 / math.sqrt(NF * n * ROWS * FS)
-    rows = facets.reshape(ROWS * COLS * 2, FS)
-    seen = observed.reshape(SLOTS * 2, SG * SG)
-    smem = pl.BlockSpec(memory_space=pltpu.SMEM)
+    hbm = pl.BlockSpec(memory_space=pltpu.HBM)
     vmem = pl.BlockSpec(memory_space=pltpu.VMEM)
     bf16 = jnp.bfloat16
     f32 = jnp.float32
@@ -371,9 +391,18 @@
             jax.ShapeDtypeStruct((ROWS * COLS * 2, FS), f32),
             jax.ShapeDtypeStruct((SLOTS * 2, SG * SG), bf16),
         ),
-        in_specs=[smem] * 6 + [vmem] * 2,
+        in_specs=[hbm] * 8,
         out_specs=(vmem, vmem),
         scratch_shapes=[
+            pltpu.SMEM((SLOTS,), jnp.int32),
+            pltpu.SMEM((SLOTS,), jnp.int32),
+            pltpu.SMEM((SLOTS,), jnp.int32),
+            pltpu.SMEM((SLOTS,), jnp.int32),
+            pltpu.SMEM(gain_real.shape, f32),
+            pltpu.SMEM(gain_imag.shape, f32),
+            pltpu.VMEM(observed.shape, bf16),
+            pltpu.VMEM(facets.shape, bf16),
+            pltpu.VMEM((ROWS * COLS * 2, FS), bf16),
             pltpu.VMEM((n, 8, LANES), jnp.int32),
             pltpu.VMEM((64, LANES), jnp.int32),
             pltpu.VMEM((64, LANES), jnp.int32),
@@ -393,12 +422,12 @@
             pltpu.VMEM((n, 2 * ROWS, LANES), bf16),
             pltpu.VMEM((HIGH * ROWS * 8, 2 * LANES), bf16),
             pltpu.VMEM((HIGH * ROWS * 8, 2 * LANES), bf16),
-            dma((n,)), dma((n,)), dma((n, nf)), dma((n, nf)), dma((n,)), dma((n,)),
+            dma((n,)), dma((n,)), dma((n, nf)), dma((n, nf)), dma((n,)), dma((n,)), dma((8,)),
         ],
         compiler_params=pltpu.CompilerParams(
             collective_id=0, has_side_effects=True, vmem_limit_bytes=48 * 1024 * 1024
         ),
-    )(sub_v, sub_u, sub_block, sub_count, gain_real, gain_imag, seen, rows)
+    )(sub_v, sub_u, sub_block, sub_count, gain_real, gain_imag, observed, facets)
     return (out.reshape(ROWS, COLS, 2, FS), res.reshape(SLOTS, 2, SG * SG))
 
 

time: 35 us -> 38.5 us (1.10)
  local copies, waits for them, and re-layouts: 4.3 us -> 7.94 us
    unnamed x12 -> x16, local copies, waits for them, and re-layouts: 0.04 us -> 5.72 us
    reshape x2 -> x0, local copies, waits for them, and re-layouts: 2.04 us -> none  [the longest x1 1.26 us: per_device(): rows = facets.reshape(ROWS * COLS * 2, FS)]
where the time goes in v4:
time: 38.5 us; the launch traced here: 38.2 us
  Pallas kernels  29.7 us (77%)
  local copies, waits for them, and re-layouts  7.94 us (21%)
  between operations  0.66 us (2%)
    pallas_call x1, Pallas kernels, per_device(): pl.pallas_call(functools.partial(kernel, n, nf, scale), out_shape=(jax.Sh...  29.7 us
    unnamed x16, local copies, waits for them, and re-layouts  5.72 us
    reshape x2, local copies, waits for them, and re-layouts, per_device(): return (out.reshape(ROWS, COLS, 2, FS), res.reshape(SLOTS, 2, SG * SG))  2.22 us

profile of v4, /device:TPU:0, one launch (start us, length us, event | category | flops | bytes accessed | tf_op | source)
XLA Modules:
  0.0 38.2 jit_solution(5147566992511592434)
XLA Ops:
  0.6 0.0 copy-start
  0.6 1.0 %copy-done = bf16[8,4,2,4096]{3,2,1,0:T(2,128)(2,1)S(1)} copy-done((bf16[8,4,2,4096]{3,2,1,0:T(2,128)(2,1)S(1)}, bf16[8,4,2,4096]{3,2,1,0:T(2,128)(2,1)}, u32[]{:S(2)}) %copy-start) | copy-done | bytes 524312
  1.7 0.0 copy-start.1
  1.7 0.8 %copy-done.1 = bf16[8,2,1024]{2,1,0:T(2,128)(2,1)S(1)} copy-done((bf16[8,2,1024]{2,1,0:T(2,128)(2,1)S(1)}, bf16[8,2,1024]{2,1,0:T(2,128)(2,1)}, u32[]{:S(2)}) %copy-start.1) | copy-done | bytes 32792
  2.4 0.0 copy-start.2
  2.4 0.7 %copy-done.2 = s32[8]{0:T(128)S(1)} copy-done((s32[8]{0:T(128)S(1)}, s32[8]{0:T(128)}, u32[]{:S(2)}) %copy-start.2) | copy-done | bytes 56
  3.1 0.0 copy-start.3
  3.1 0.7 %copy-done.3 = s32[8]{0:T(128)S(1)} copy-done((s32[8]{0:T(128)S(1)}, s32[8]{0:T(128)}, u32[]{:S(2)}) %copy-start.3) | copy-done | bytes 56
  3.7 0.0 copy-start.4
  3.7 0.7 %copy-done.4 = s32[8]{0:T(128)S(1)} copy-done((s32[8]{0:T(128)S(1)}, s32[8]{0:T(128)}, u32[]{:S(2)}) %copy-start.4) | copy-done | bytes 56
  4.4 0.0 copy-start.5
  4.4 0.7 %copy-done.5 = s32[8]{0:T(128)S(1)} copy-done((s32[8]{0:T(128)S(1)}, s32[8]{0:T(128)}, u32[]{:S(2)}) %copy-start.5) | copy-done | bytes 56
  5.1 0.0 copy-start.6
  5.1 0.7 %copy-done.6 = f32[128]{0:T(128)S(1)} copy-done((f32[128]{0:T(128)S(1)}, f32[128]{0:T(128)}, u32[]{:S(2)}) %copy-start.6) | copy-done | bytes 536
  5.7 0.0 copy-start.7
  5.7 0.7 %copy-done.7 = f32[128]{0:T(128)S(1)} copy-done((f32[128]{0:T(128)S(1)}, f32[128]{0:T(128)}, u32[]{:S(2)}) %copy-start.7) | copy-done | bytes 536
  6.4 29.7 %shard_map.95 = (f32[64,4096]{1,0:T(8,128)S(1)}, bf16[16,1024]{1,0:T(8,128)(2,1)S(1)}) custom-call(s32[8]{0:T(128)S(1)} %copy-done.2, s32[8]{0:T(128)S(1)} %copy-done.3, s32[8]{0:T(128)S(1)} %copy-done.4, s32[8]{0:T(128)S(1)} %copy-done.5, f32[128]{0:T(128)S(1)} %copy-done.6, f32[128]{0:T(128)S(1)} %copy-done.7, bf16[8,2,1024]{2,1,0:T(2,128)(2,1)S(1)} %copy-done.1, ...), custom_call_target="tpu_custom_call" | custom-call | tf_op jit(solution)/shard_map/pallas_call | solution.py:388
  36.0 1.6 %reshape.10 = f32[8,4,2,4096]{3,2,1,0:T(2,128)} reshape(f32[64,4096]{1,0:T(8,128)S(1)} %get-tuple-element.4) | data formatting | bytes 2097152 | tf_op jit(solution)/shard_map/reshape | solution.py:431
  37.6 0.6 %reshape.11 = bf16[8,2,1024]{2,1,0:T(2,128)(2,1)} reshape(bf16[16,1024]{1,0:T(8,128)(2,1)S(1)} %get-tuple-element.5) | data formatting | bytes 65536 | tf_op jit(solution)/shard_map/reshape | solution.py:431
Async XLA Ops:
  0.6 1.0 %copy-start = (bf16[8,4,2,4096]{3,2,1,0:T(2,128)(2,1)S(1)}, bf16[8,4,2,4096]{3,2,1,0:T(2,128)(2,1)}, u32[]{:S(2)}) copy-start(bf16[8,4,2,4096]{3,2,1,0:T(2,128)(2,1)} %facet_raw.1) | copy-start | bytes 1572868
  1.7 0.8 %copy-start.1 = (bf16[8,2,1024]{2,1,0:T(2,128)(2,1)S(1)}, bf16[8,2,1024]{2,1,0:T(2,128)(2,1)}, u32[]{:S(2)}) copy-start(bf16[8,2,1024]{2,1,0:T(2,128)(2,1)} %seen_raw.1) | copy-start | bytes 98308
  2.4 0.7 %copy-start.2 = (s32[8]{0:T(128)S(1)}, s32[8]{0:T(128)}, u32[]{:S(2)}) copy-start(s32[8]{0:T(128)} %v_raw.1) | copy-start | bytes 100
  3.1 0.7 %copy-start.3 = (s32[8]{0:T(128)S(1)}, s32[8]{0:T(128)}, u32[]{:S(2)}) copy-start(s32[8]{0:T(128)} %u_raw.1) | copy-start | bytes 100
  3.7 0.7 %copy-start.4 = (s32[8]{0:T(128)S(1)}, s32[8]{0:T(128)}, u32[]{:S(2)}) copy-start(s32[8]{0:T(128)} %block_raw.1) | copy-start | bytes 100
  4.4 0.7 %copy-start.5 = (s32[8]{0:T(128)S(1)}, s32[8]{0:T(128)}, u32[]{:S(2)}) copy-start(s32[8]{0:T(128)} %count_raw.1) | copy-start | bytes 100
  5.1 0.7 %copy-start.6 = (f32[128]{0:T(128)S(1)}, f32[128]{0:T(128)}, u32[]{:S(2)}) copy-start(f32[128]{0:T(128)} %gain_re_raw.1) | copy-start | bytes 1540
  5.7 0.7 %copy-start.7 = (f32[128]{0:T(128)S(1)}, f32[128]{0:T(128)}, u32[]{:S(2)}) copy-start(f32[128]{0:T(128)} %gain_im_raw.1) | copy-start | bytes 1540

commit v5 on v4

--- a/solution.py
+++ b/solution.py
@@ -99,8 +99,8 @@
     out_ref, res_ref,
     v_ref, u_ref, block_ref, count_ref, gain_re_ref, gain_im_ref, seen_ref, facet_four,
     facet_ref, freq, distance, quarter, low_even, low_odd, one_even, one_odd, two_even, two_odd, row_table,
-    seen_cells, product_even, product_odd, strip_out, strip, lift, lifted, spread_even, spread_odd,
-    v_send, v_recv, s_send, s_recv, l_send, l_recv, in_sem,
+    seen_cells, product_even, product_odd, strip_out, strip, model, lift, lifted, spread_even, spread_odd,
+    v_send, v_recv, s_send, s_recv, m_send, m_recv, l_send, l_recv, in_sem,
 ):
     me = lax.axis_index("base")
     mf = lax.axis_index("facet")
@@ -120,8 +120,7 @@
     barrier = pltpu.get_barrier_semaphore()
 
     def greet(k, _):
-        for j in range(nf):
-            pl.semaphore_signal(barrier, inc=1, device_id=device(k, j), device_id_type=MESH)
+        pl.semaphore_signal(barrier, inc=1, device_id=device(k, 0), device_id_type=MESH)
         return 0
 
     lax.fori_loop(1, n, greet, 0)
@@ -146,7 +145,7 @@
             both += [facet_four[t, b].astype(jnp.float32) for b in range(COLS)]
         facet_ref[pl.ds(r * 8, 16), :] = jnp.concatenate(both, 0).astype(jnp.bfloat16)
 
-    pl.semaphore_wait(barrier, n * nf - 1)
+    pl.semaphore_wait(barrier, n - 1 + nf - 1)
 
     def v_copy(k, slot):
         return pltpu.make_async_remote_copy(
@@ -171,12 +170,12 @@
     turn = (sub // SG - lane // ROWS % 2) * QUARTER
     first = (FS - n * ROWS) // 2 + lane // (2 * ROWS) * ROWS + lane % ROWS
 
+    place = first + (mf + 2) * FS
+
     def fill_rows(s, _):
-        u = sub % SG + u_ref[s]
-        for a in range(nf):
-            row_table[a, pl.ds(pl.multiple_of(s * 2 * SG, 2 * SG), 2 * SG), :] = cos_turns(
-                u * (first + (a + 2) * FS) + turn
-            ).astype(jnp.bfloat16)
+        row_table[pl.ds(pl.multiple_of(s * 2 * SG, 2 * SG), 2 * SG), :] = cos_turns(
+            (sub % SG + u_ref[s]) * place + turn
+        ).astype(jnp.bfloat16)
         return 0
 
     lax.fori_loop(0, SLOTS, fill_rows, 0)
@@ -196,11 +195,16 @@
         placed = jnp.where(owner == s, picked[s * 2 * SG : (s + 1) * 2 * SG], placed)
     seen_cells[...] = placed
 
-    def strip_copy(k, j, from_facet, from_base):
+    def strip_copy(k, slot):
         return pltpu.make_async_remote_copy(
-            src_ref=strip_out.at[k], dst_ref=strip.at[from_facet, from_base],
-            send_sem=s_send.at[k, j], recv_sem=s_recv.at[k, j],
-            device_id=device(k, j), device_id_type=MESH,
+            src_ref=strip_out.at[k], dst_ref=strip.at[slot], send_sem=s_send.at[k],
+            recv_sem=s_recv.at[k], device_id=device(k, 0), device_id_type=MESH,
+        )
+
+    def model_copy(j, slot):
+        return pltpu.make_async_remote_copy(
+            src_ref=model.at[mf], dst_ref=model.at[slot], send_sem=m_send.at[j],
+            recv_sem=m_recv.at[j], device_id=device(0, j), device_id_type=MESH,
         )
 
     def multiply(low, product):
@@ -226,14 +230,11 @@
     def send_strip(k):
         @pl.when(k == 0)
         def _():
-            strip[mf, me] = strip_out[k]
+            strip[me] = strip_out[k]
 
         @pl.when(k > 0)
         def _():
-            strip_copy(k, 0, mf, me).start()
-
-        for j in range(1, nf):
-            strip_copy(k, j, mf, me).start()
+            strip_copy(k, me).start()
 
     def take_v(k):
         v_copy(n - k, lax.rem(me + k, n)).wait_recv()
@@ -262,27 +263,26 @@
     weight = per_lane([count_ref[s] for s in range(SLOTS)], half).astype(jnp.float32) / CMAX
     seen = seen_cells[...]
 
-    def take_strip(k, j):
-        strip_copy(k, j, lax.rem(mf + nf - j, nf), lax.rem(me + n - k, n)).wait_recv()
-
-    def take_strips(k, _):
-        for j in range(nf):
-            take_strip(k, j)
-        return 0
-
+    def take_strip(k, _):
+        strip_copy(k, lax.rem(me + n - k, n)).wait_recv()
+        return 0
+
+    lax.fori_loop(1, n, take_strip, 0)
+
+    crossed = jnp.dot(
+        row_table[...], strip[...].reshape(wide, LANES), preferred_element_type=jnp.float32
+    )
+    part = jnp.zeros((2 * SG, LANES), jnp.float32)
+    for s in range(SLOTS):
+        part = jnp.where(owner == s, crossed[s * 2 * SG : (s + 1) * 2 * SG], part)
+    model[mf] = (part * scale).astype(jnp.bfloat16)
     for j in range(1, nf):
-        take_strip(0, j)
-    lax.fori_loop(1, n, take_strips, 0)
-
-    crossed = jnp.zeros((SLOTS * 2 * SG, LANES), jnp.float32)
-    for a in range(nf):
-        crossed = crossed + jnp.dot(
-            row_table[a], strip[a].reshape(wide, LANES), preferred_element_type=jnp.float32
-        )
-    whole = jnp.zeros((2 * SG, LANES), jnp.float32)
-    for s in range(SLOTS):
-        whole = jnp.where(owner == s, crossed[s * 2 * SG : (s + 1) * 2 * SG], whole)
-    whole = whole * scale
+        model_copy(j, mf).start()
+    for j in range(1, nf):
+        model_copy(j, lax.rem(mf + nf - j, nf)).wait_recv()
+    whole = model[0].astype(jnp.float32)
+    for j in range(1, nf):
+        whole = whole + model[j].astype(jnp.float32)
     model_re = whole[:SG]
     model_im = whole[SG:]
     diff_re = seen[:SG] - (gain_re * model_re - gain_im * model_im)
@@ -295,7 +295,7 @@
         [jnp.where(owner == s, residual, 0.0).astype(jnp.bfloat16) for s in range(SLOTS)], 0
     )
     raised = lax.dot_general(
-        row_table[mf], blocks, (((0,), (0,)), ((), ())), preferred_element_type=jnp.float32
+        row_table[...], blocks, (((0,), (0,)), ((), ())), preferred_element_type=jnp.float32
     )
     lift[...] = raised.astype(jnp.bfloat16).reshape(n, 2 * ROWS, LANES)
 
@@ -365,13 +365,12 @@
     def drain(k, _):
         v_copy(k, me).wait_send()
         lift_copy(k, me).wait_send()
-        for j in range(nf):
-            strip_copy(k, j, mf, me).wait_send()
+        strip_copy(k, me).wait_send()
         return 0
 
     lax.fori_loop(1, n, drain, 0)
     for j in range(1, nf):
-        strip_copy(0, j, mf, me).wait_send()
+        model_copy(j, mf).wait_send()
 
 
 def per_device(facets, observed, sub_u, sub_v, sub_block, sub_count, gain_real, gain_imag):
@@ -412,20 +411,22 @@
             pltpu.VMEM((n // 2, HIGH, 8, LANES), f32),
             pltpu.VMEM((n // 2 + 1, HIGH, 8, LANES), f32),
             pltpu.VMEM((n // 2, HIGH, 8, LANES), f32),
-            pltpu.VMEM((nf, SLOTS * 2 * SG, n * 2 * ROWS), bf16),
+            pltpu.VMEM((SLOTS * 2 * SG, n * 2 * ROWS), bf16),
             pltpu.VMEM((2 * SG, LANES), f32),
             pltpu.VMEM((HIGH * ROWS * 8, 2 * LANES), f32),
             pltpu.VMEM((HIGH * ROWS * 8, 2 * LANES), f32),
             pltpu.VMEM((n, 2 * ROWS, LANES), bf16),
-            pltpu.VMEM((nf, n, 2 * ROWS, LANES), bf16),
+            pltpu.VMEM((n, 2 * ROWS, LANES), bf16),
+            pltpu.VMEM((nf, 2 * SG, LANES), bf16),
             pltpu.VMEM((n, 2 * ROWS, LANES), bf16),
             pltpu.VMEM((n, 2 * ROWS, LANES), bf16),
             pltpu.VMEM((HIGH * ROWS * 8, 2 * LANES), bf16),
             pltpu.VMEM((HIGH * ROWS * 8, 2 * LANES), bf16),
-            dma((n,)), dma((n,)), dma((n, nf)), dma((n, nf)), dma((n,)), dma((n,)), dma((8,)),
+            dma((n,)), dma((n,)), dma((n,)), dma((n,)), dma((nf,)), dma((nf,)), dma((n,)), dma((n,)),
+            dma((8,)),
         ],
         compiler_params=pltpu.CompilerParams(
-            collective_id=0, has_side_effects=True, vmem_limit_bytes=48 * 1024 * 1024
+            collective_id=0, has_side_effects=True, vmem_limit_bytes=62 * 1024 * 1024
         ),
     )(sub_v, sub_u, sub_block, sub_count, gain_real, gain_imag, observed, facets)
     return (out.reshape(ROWS, COLS, 2, FS), res.reshape(SLOTS, 2, SG * SG))

time: 38.5 us -> 35.3 us (0.917)
  local copies, waits for them, and re-layouts: 7.94 us -> 3.46 us
  Pallas kernels: 29.7 us -> 31 us
    unnamed x16 -> x2, local copies, waits for them, and re-layouts: 5.72 us -> 0.01 us
    pallas_call x1, Pallas kernels: 29.7 us -> 31 us  [per_device(): pl.pallas_call(functools.partial(kernel, n, nf, scale), out_shape=(jax.Sh...]
    reshape x2, local copies, waits for them, and re-layouts: 2.22 us -> 3.45 us  [per_device(): return (out.reshape(ROWS, COLS, 2, FS), res.reshape(SLOTS, 2, SG * SG))]
where the time goes in v5:
time: 35.3 us; the launch traced here: 35.1 us
  Pallas kernels  31 us (88%)
  local copies, waits for them, and re-layouts  3.46 us (10%)
  between operations  0.65 us (2%)
    pallas_call x1, Pallas kernels, per_device(): pl.pallas_call(functools.partial(kernel, n, nf, scale), out_shape=(jax.Sh...  31 us
    reshape x2, local copies, waits for them, and re-layouts, per_device(): return (out.reshape(ROWS, COLS, 2, FS), res.reshape(SLOTS, 2, SG * SG))  3.45 us

profile of v5, /device:TPU:0, one launch (start us, length us, event | category | flops | bytes accessed | tf_op | source)
XLA Modules:
  0.0 35.1 jit_solution(2678843586293973481)
XLA Ops:
  0.6 31.0 %shard_map.95 = (f32[64,4096]{1,0:T(8,128)}, bf16[16,1024]{1,0:T(8,128)(2,1)}) custom-call(s32[8]{0:T(128)} %v_raw.1, s32[8]{0:T(128)} %u_raw.1, s32[8]{0:T(128)} %block_raw.1, s32[8]{0:T(128)} %count_raw.1, f32[128]{0:T(128)} %gain_re_raw.1, f32[128]{0:T(128)} %gain_im_raw.1, bf16[8,2,1024]{2,1,0:T(2,128)(2,1)} %seen_raw.1, bf16[8,4,2,4096]{3,2,1,0:T(2,128)(2,1)} %facet_raw.1), custom_call_target="tpu_custom_call" | custom-call | tf_op jit(solution)/shard_map/pallas_call | solution.py:387
  31.7 0.0 copy-start
  31.7 2.8 %reshape.10 = f32[8,4,2,4096]{3,2,1,0:T(2,128)} reshape(f32[64,4096]{1,0:T(8,128)} %get-tuple-element.4) | data formatting | bytes 2097152 | tf_op jit(solution)/shard_map/reshape | solution.py:432
  34.5 0.0 copy-done
  34.5 0.6 %reshape.11 = bf16[8,2,1024]{2,1,0:T(2,128)(2,1)} reshape(bf16[16,1024]{1,0:T(8,128)(2,1)S(1)} %copy-done) | data formatting | bytes 65536 | tf_op jit(solution)/shard_map/reshape | solution.py:432
Async XLA Ops:
  31.7 2.8 %copy-start = (bf16[16,1024]{1,0:T(8,128)(2,1)S(1)}, bf16[16,1024]{1,0:T(8,128)(2,1)}, u32[]{:S(2)}) copy-start(bf16[16,1024]{1,0:T(8,128)(2,1)} %get-tuple-element.5) | copy-start | bytes 98308

commit v6 on v5

v6 whole, which is shorter than its diff:
```python
import functools
import math

import jax
import jax.numpy as jnp
from jax import lax
from jax.experimental import pallas as pl
from jax.experimental.pallas import tpu as pltpu
from jax.sharding import PartitionSpec as P

FS = 4096
NPIX = 32768
SG = 32
NF = 16
CMAX = 4096
QUARTER = NPIX // 4
MESH = pl.DeviceIdType.MESH

LOW = 512
HIGH = FS // LOW
COLS = 4
ROWS = 8
SLOTS = 8
LANES = SLOTS * SG
HALF = LANES // 2
STEP = 16


def cos_turns(turns):
    away = jnp.abs(((turns + NPIX // 2) & (NPIX - 1)) - NPIX // 2)
    x = (QUARTER - away).astype(jnp.float32) * (2.0 * math.pi / NPIX)
    x2 = x * x
    tail = -1.0 / 39916800
    for term in (362880, -5040, 120, -6):
        tail = tail * x2 + 1.0 / term
    return x + x * (x2 * tail)


def iota(shape, dim):
    return lax.broadcasted_iota(jnp.int32, shape, dim)


def per_lane(values, shape):
    owner = iota(shape, len(shape) - 1) // SG
    out = jnp.full(shape, values[0])
    for s in range(1, SLOTS):
        out = jnp.where(owner == s, values[s], out)
    return out


def turned(one, two, c, s):
    return one * c + two * s, two * c - one * s


def phase_plan():
    shape = (64, LANES)
    group = iota(shape, 0) // 8
    line = iota(shape, 0) % 8
    facet = (line // 2 + 2) * FS
    shift = jnp.where(line == 0, 8, 64 << line)
    distance = jnp.where(group < 2, line, jnp.where(group < 4, line * STEP, facet))
    distance = jnp.where(group < 6, distance, shift)
    sine = (group == 1) | (group == 3) | (group == 7)
    quarter = jnp.where(group == 4, -(line % 2), jnp.where(group == 5, 1 - line % 2, 0))
    return distance, jnp.where(sine, -1, quarter) * QUARTER


def fill_tables(f, distance, quarter, low, one, two):
    table = cos_turns(jnp.concatenate([f] * 8, 0) * distance[...] + quarter[...])

    def by(i):
        return table[48 + i : 49 + i], table[56 + i : 57 + i]

    def add(pair, turn):
        return pair[0] * turn[0] - pair[1] * turn[1], pair[1] * turn[0] + pair[0] * turn[1]

    fine = (table[0:8], table[8:16])
    more = add(fine, by(0))
    fine = tuple(jnp.concatenate([x, y], 0) for x, y in zip(fine, more))
    steps = [(table[16:24], table[24:32])]
    steps.append(add(steps[0], by(1)))
    steps += [add(step, by(2)) for step in steps[:2]]
    lines = [(table[32:40], table[40:48])]
    for i in range(3):
        lines += [turned(*line, *by(3 + i)) for line in lines]
    for h in range(HIGH):
        one[h] = lines[h][0]
        two[h] = lines[h][1]
    for i in range(LOW // STEP):
        step = tuple(x[i % 8 : i % 8 + 1] for x in steps[i // 8])
        cos, sin = add(fine, step)
        rows = pl.ds(i * STEP, STEP)
        low[rows, 0:LANES] = cos.astype(jnp.bfloat16)
        low[rows, LANES : 2 * LANES] = sin.astype(jnp.bfloat16)


def kernel(
    n, nf, scale,
    v_raw, u_raw, block_raw, count_raw, gain_re_raw, gain_im_raw, seen_raw, facet_raw,
    out_ref, res_ref,
    v_ref, u_ref, block_ref, count_ref, gain_re_ref, gain_im_ref, seen_ref, facet_four,
    facet_ref, freq, distance, quarter, low, one, two, row_table,
    seen_cells, product, strip_out, strip, model, blocks, lift, lifted, spread, image,
    v_send, v_recv, s_send, s_recv, m_send, m_recv, l_send, l_recv, in_sem,
):
    me = lax.axis_index("base")
    mf = lax.axis_index("facet")
    pairs = n // 2

    def device(k, j):
        return {"base": lax.rem(me + k, n), "facet": lax.rem(mf + j, nf)}

    raw = [v_raw, facet_raw, seen_raw, u_raw, block_raw, count_raw, gain_re_raw, gain_im_raw]
    held = [v_ref, facet_four, seen_ref, u_ref, block_ref, count_ref, gain_re_ref, gain_im_ref]
    loads = [
        pltpu.make_async_copy(src, dst, in_sem.at[i]) for i, (src, dst) in enumerate(zip(raw, held))
    ]
    for load in loads:
        load.start()

    barrier = pltpu.get_barrier_semaphore()

    def greet(k, _):
        pl.semaphore_signal(barrier, inc=1, device_id=device(k, 0), device_id_type=MESH)
        return 0

    lax.fori_loop(1, n, greet, 0)
    for j in range(1, nf):
        pl.semaphore_signal(barrier, inc=1, device_id=device(0, j), device_id_type=MESH)

    loads[0].wait()
    freq[me] = per_lane([v_ref[s] for s in range(SLOTS)], (8, LANES)) + iota((8, LANES), 1) % SG
    distance[...], quarter[...] = phase_plan()

    loads[1].wait()
    for r in range(0, ROWS, 2):
        both = []
        for t in (r, r + 1):
            both += [facet_four[t, b].astype(jnp.float32) for b in range(COLS)]
        facet_ref[pl.ds(r * 8, 16), :] = jnp.concatenate(both, 0).astype(jnp.bfloat16)

    pl.semaphore_wait(barrier, n - 1 + nf - 1)

    def v_copy(k, slot):
        return pltpu.make_async_remote_copy(
            src_ref=freq.at[me], dst_ref=freq.at[slot], send_sem=v_send.at[k],
            recv_sem=v_recv.at[k], device_id=device(k, 0), device_id_type=MESH,
        )

    def send_v(k, _):
        v_copy(k, me).start()
        return 0

    lax.fori_loop(1, n, send_v, 0)

    for load in loads[2:]:
        load.wait()

    wide = n * 2 * ROWS
    lane = iota((2 * SG, wide), 1)
    sub = iota((2 * SG, wide), 0)
    turn = (sub // SG - lane // ROWS % 2) * QUARTER
    first = (FS - n * ROWS) // 2 + lane // (2 * ROWS) * ROWS + lane % ROWS

    place = first + (mf + 2) * FS

    def fill_rows(s, _):
        row_table[pl.ds(pl.multiple_of(s * 2 * SG, 2 * SG), 2 * SG), :] = cos_turns(
            (sub % SG + u_ref[s]) * place + turn
        ).astype(jnp.bfloat16)
        return 0

    lax.fori_loop(0, SLOTS, fill_rows, 0)

    group = iota((2 * SG, LANES), 1) // SG
    cells = SG * SG
    same = iota((SG, cells), 1) // SG == iota((SG, cells), 0)
    tall = []
    for s in range(SLOTS):
        seen = seen_ref[s].astype(jnp.float32)
        tall += [jnp.where(same, seen[i : i + 1], 0.0).astype(jnp.bfloat16) for i in range(2)]
    tall = jnp.concatenate(tall, 0)
    pick = (iota((cells, LANES), 0) % SG == iota((cells, LANES), 1) % SG).astype(jnp.float32)
    picked = jnp.dot(tall, pick.astype(jnp.bfloat16), preferred_element_type=jnp.float32)
    placed = jnp.zeros((2 * SG, LANES), jnp.float32)
    for s in range(SLOTS):
        placed = jnp.where(group == s, picked[s * 2 * SG : (s + 1) * 2 * SG], placed)
    seen_cells[...] = placed

    def strip_copy(half, k, slot):
        return pltpu.make_async_remote_copy(
            src_ref=strip_out.at[half, k], dst_ref=strip.at[half, slot],
            send_sem=s_send.at[half, k], recv_sem=s_recv.at[half, k], device_id=device(k, 0),
            device_id_type=MESH,
        )

    def model_copy(half, j, slot):
        return pltpu.make_async_remote_copy(
            src_ref=model.at[half, mf], dst_ref=model.at[half, slot],
            send_sem=m_send.at[half, j], recv_sem=m_recv.at[half, j], device_id=device(0, j),
            device_id_type=MESH,
        )

    def lift_copy(half, k, slot):
        return pltpu.make_async_remote_copy(
            src_ref=lift.at[half, lax.rem(me + k, n)], dst_ref=lifted.at[half, slot],
            send_sem=l_send.at[half, k], recv_sem=l_recv.at[half, k], device_id=device(k, 0),
            device_id_type=MESH,
        )

    def take_v(k):
        v_copy(n - k, lax.rem(me + k, n)).wait_recv()

    def degrid(half, i):
        k = 2 * i
        g = lax.rem(me + k, n)
        g_next = lax.rem(me + k + 1, n)
        if half == 0:
            pl.when(k > 0)(lambda: take_v(k))
            take_v(k + 1)
        at = half * pairs + i
        part = slice(half * HALF, (half + 1) * HALF)
        f = jnp.concatenate([freq[g][:, part], freq[g_next][:, part]], 1)
        fill_tables(f, distance, quarter, low.at[at], one.at[at], two.at[at])
        tall = jnp.concatenate([facet_ref[:, h * LOW : (h + 1) * LOW] for h in range(HIGH)], 0)
        product[...] = jnp.dot(tall, low[at], preferred_element_type=jnp.float32)
        lines_re = []
        lines_im = []
        for r in range(ROWS):
            total_re = jnp.zeros((8, LANES), jnp.float32)
            total_im = jnp.zeros((8, LANES), jnp.float32)
            for h in range(HIGH):
                rows = pl.ds((h * ROWS + r) * 8, 8)
                part_cos = product[rows, 0:LANES]
                part_sin = product[rows, LANES : 2 * LANES]
                total_re = total_re + (part_cos * one[at, h] + part_sin * two[at, h])
                total_im = total_im + (part_cos * two[at, h] - part_sin * one[at, h])
            lines_re.append(jnp.sum(total_re, 0, keepdims=True))
            lines_im.append(jnp.sum(total_im, 0, keepdims=True))
        chunk = jnp.concatenate(lines_re + lines_im, 0).astype(jnp.bfloat16)
        strip_out[half, k] = chunk[:, :HALF]
        strip_out[half, k + 1] = chunk[:, HALF:]

        @pl.when(k == 0)
        def _():
            strip[half, me] = strip_out[half, 0]

        @pl.when(k > 0)
        def _():
            strip_copy(half, k, me).start()

        strip_copy(half, k + 1, me).start()

    half_rows = SLOTS // 2 * 2 * SG
    owner = iota((2 * SG, HALF), 1) // SG

    def sum_rows(half):
        def take(k, _):
            strip_copy(half, k, lax.rem(me + n - k, n)).wait_recv()
            return 0

        lax.fori_loop(1, n, take, 0)
        crossed = jnp.dot(
            row_table[half * half_rows : (half + 1) * half_rows, :],
            strip[half].reshape(wide, HALF),
            preferred_element_type=jnp.float32,
        )
        part = jnp.zeros((2 * SG, HALF), jnp.float32)
        for s in range(SLOTS // 2):
            part = jnp.where(owner == s, crossed[s * 2 * SG : (s + 1) * 2 * SG], part)
        model[half, mf] = (part * scale).astype(jnp.bfloat16)
        for j in range(1, nf):
            model_copy(half, j, mf).start()

    def raise_rows(half):
        full = (SG, LANES)
        part = slice(half * HALF, (half + 1) * HALF)
        gain_re = per_lane([gain_re_ref[block_ref[s]] for s in range(SLOTS)], full)[:, part]
        gain_im = per_lane([gain_im_ref[block_ref[s]] for s in range(SLOTS)], full)[:, part]
        weight = per_lane([count_ref[s] for s in range(SLOTS)], full)[:, part]
        weight = weight.astype(jnp.float32) / CMAX
        seen = seen_cells[:, part]
        for j in range(1, nf):
            model_copy(half, j, lax.rem(mf + nf - j, nf)).wait_recv()
        whole = model[half, 0].astype(jnp.float32)
        for j in range(1, nf):
            whole = whole + model[half, j].astype(jnp.float32)
        model_re = whole[:SG]
        model_im = whole[SG:]
        diff_re = seen[:SG] - (gain_re * model_re - gain_im * model_im)
        diff_im = seen[SG:] - (gain_re * model_im + gain_im * model_re)
        res_re = weight * (gain_re * diff_re + gain_im * diff_im)
        res_im = weight * (gain_re * diff_im - gain_im * diff_re)
        residual = jnp.concatenate([res_re, res_im], 0)
        blocks[half] = jnp.concatenate(
            [
                jnp.where(owner == s, residual, 0.0).astype(jnp.bfloat16)
                for s in range(SLOTS // 2)
            ],
            0,
        )
        raised = lax.dot_general(
            row_table[half * half_rows : (half + 1) * half_rows, :],
            blocks[half],
            (((0,), (0,)), ((), ())),
            preferred_element_type=jnp.float32,
        )
        lift[half] = raised.astype(jnp.bfloat16).reshape(n, 2 * ROWS, HALF)

        def send(k, _):
            lift_copy(half, k, me).start()
            return 0

        lax.fori_loop(1, n, send, 0)
        lifted[half, me] = lift[half, me]

    def grid(half, i):
        k = 2 * i
        g = lax.rem(me + k, n)
        g_next = lax.rem(me + k + 1, n)
        pl.when(k > 0)(lambda: lift_copy(half, n - k, g).wait_recv())
        lift_copy(half, n - k - 1, g_next).wait_recv()
        at = half * pairs + i
        value = jnp.concatenate([lifted[half, g], lifted[half, g_next]], 1)
        value = value.astype(jnp.float32) * scale
        for h in range(HIGH):
            for r in range(0, ROWS, 2):
                by_cos = []
                by_sin = []
                for t in (r, r + 1):
                    re = value[t : t + 1]
                    im = value[ROWS + t : ROWS + t + 1]
                    by_cos.append(re * one[at, h] + im * two[at, h])
                    by_sin.append(re * two[at, h] - im * one[at, h])
                rows = pl.ds((h * ROWS + r) * 8, 16)
                spread[rows, 0:LANES] = jnp.concatenate(by_cos, 0).astype(jnp.bfloat16)
                spread[rows, LANES : 2 * LANES] = jnp.concatenate(by_sin, 0).astype(jnp.bfloat16)
        term = lax.dot_general(
            spread[...], low[at], (((1,), (1,)), ((), ())), preferred_element_type=jnp.float32
        )
        for h in range(HIGH):
            image[:, pl.ds(h * LOW, LOW)] += term[h * 8 * ROWS : (h + 1) * 8 * ROWS]

    def loop(first, last, step, half):
        def body(i, _):
            step(half, i)
            return 0

        lax.fori_loop(first, last, body, 0)

    middle = (pairs + 1) // 2
    loop(0, pairs, degrid, 0)
    loop(0, middle, degrid, 1)
    sum_rows(0)
    loop(middle, pairs, degrid, 1)
    raise_rows(0)
    sum_rows(1)
    image[...] = jnp.zeros(image.shape, jnp.float32)
    loop(0, middle, grid, 0)
    raise_rows(1)
    loop(middle, pairs, grid, 0)

    grow = (iota((HALF, cells), 0) % SG == iota((HALF, cells), 1) % SG).astype(jnp.float32)
    grown = jnp.dot(
        blocks[...].reshape(2 * half_rows, HALF),
        grow.astype(jnp.bfloat16),
        preferred_element_type=jnp.float32,
    )
    for s in range(SLOTS):
        lines = [
            jnp.sum(jnp.where(same, grown[i * SG : (i + 1) * SG], 0.0), 0, keepdims=True)
            for i in (2 * s, 2 * s + 1)
        ]
        res_ref[s] = jnp.concatenate(lines, 0).astype(jnp.bfloat16)

    loop(0, pairs, grid, 1)
    for r in range(ROWS):
        for b in range(COLS):
            line = r * 8 + b * 2
            out_ref[r, b] = image[line : line + 2, :]

    def drain(k, _):
        v_copy(k, me).wait_send()
        for half in range(2):
            strip_copy(half, k, me).wait_send()
            lift_copy(half, k, me).wait_send()
        return 0

    lax.fori_loop(1, n, drain, 0)
    for half in range(2):
        for j in range(1, nf):
            model_copy(half, j, mf).wait_send()


def per_device(facets, observed, sub_u, sub_v, sub_block, sub_count, gain_real, gain_imag):
    n = lax.axis_size("base")
    nf = lax.axis_size("facet")
    assert facets.shape == (ROWS, COLS, 2, FS) and nf * COLS == NF and n % 2 == 0
    assert observed.shape == (SLOTS, 2, SG * SG)
    scale = 1.0 / math.sqrt(NF * n * ROWS * FS)
    hbm = pl.BlockSpec(memory_space=pltpu.HBM)
    vmem = pl.BlockSpec(memory_space=pltpu.VMEM)
    bf16 = jnp.bfloat16
    f32 = jnp.float32
    dma = pltpu.SemaphoreType.DMA
    return pl.pallas_call(
        functools.partial(kernel, n, nf, scale),
        out_shape=(
            jax.ShapeDtypeStruct(facets.shape, f32),
            jax.ShapeDtypeStruct(observed.shape, bf16),
        ),
        in_specs=[hbm] * 8,
        out_specs=(vmem, vmem),
        scratch_shapes=[
            pltpu.SMEM((SLOTS,), jnp.int32),
            pltpu.SMEM((SLOTS,), jnp.int32),
            pltpu.SMEM((SLOTS,), jnp.int32),
            pltpu.SMEM((SLOTS,), jnp.int32),
            pltpu.SMEM(gain_real.shape, f32),
            pltpu.SMEM(gain_imag.shape, f32),
            pltpu.VMEM(observed.shape, bf16),
            pltpu.VMEM(facets.shape, bf16),
            pltpu.VMEM((ROWS * COLS * 2, FS), bf16),
            pltpu.VMEM((n, 8, LANES), jnp.int32),
            pltpu.VMEM((64, LANES), jnp.int32),
            pltpu.VMEM((64, LANES), jnp.int32),
            pltpu.VMEM((n, LOW, 2 * LANES), bf16),
            pltpu.VMEM((n, HIGH, 8, LANES), f32),
            pltpu.VMEM((n, HIGH, 8, LANES), f32),
            pltpu.VMEM((SLOTS * 2 * SG, n * 2 * ROWS), bf16),
            pltpu.VMEM((2 * SG, LANES), f32),
            pltpu.VMEM((HIGH * ROWS * 8, 2 * LANES), f32),
            pltpu.VMEM((2, n, 2 * ROWS, HALF), bf16),
            pltpu.VMEM((2, n, 2 * ROWS, HALF), bf16),
            pltpu.VMEM((2, nf, 2 * SG, HALF), bf16),
            pltpu.VMEM((2, SLOTS // 2 * 2 * SG, HALF), bf16),
            pltpu.VMEM((2, n, 2 * ROWS, HALF), bf16),
            pltpu.VMEM((2, n, 2 * ROWS, HALF), bf16),
            pltpu.VMEM((HIGH * ROWS * 8, 2 * LANES), bf16),
            pltpu.VMEM((ROWS * COLS * 2, FS), f32),
            dma((n,)), dma((n,)), dma((2, n)), dma((2, n)), dma((2, nf)), dma((2, nf)),
            dma((2, n)), dma((2, n)), dma((8,)),
        ],
        compiler_params=pltpu.CompilerParams(
            collective_id=0, has_side_effects=True, vmem_limit_bytes=62 * 1024 * 1024
        ),
    )(sub_v, sub_u, sub_block, sub_count, gain_real, gain_imag, observed, facets)


def solution(mesh):
    in_specs = (
        P("base", "facet", None, None),
        P("base", None, None),
        P("base"),
        P("base"),
        P("base"),
        P("base"),
        P(),
        P(),
    )
    out_specs = (P("base", "facet", None, None), P("base", None, None))
    return jax.shard_map(
        per_device, mesh=mesh, in_specs=in_specs, out_specs=out_specs, check_vma=False
    )
```

time: 35.3 us -> 34.3 us (0.972)
  local copies, waits for them, and re-layouts: 3.46 us -> 2.93 us
  Pallas kernels: 31 us -> 30.5 us
    reshape x2 -> x0, local copies, waits for them, and re-layouts: 3.45 us -> none  [per_device(): return (out.reshape(ROWS, COLS, 2, FS), res.reshape(SLOTS, 2, SG * SG))]
    unnamed x2 -> x4, local copies, waits for them, and re-layouts: 0.01 us -> 2.93 us
    pallas_call x1, Pallas kernels: 31 us -> 30.5 us  [per_device(): pl.pallas_call(functools.partial(kernel, n, nf, scale), out_shape=(jax.Sh...]
where the time goes in v6:
time: 34.3 us; the launch traced here: 34.1 us
  Pallas kernels  30.5 us (89%)
  local copies, waits for them, and re-layouts  2.93 us (9%)
  between operations  0.65 us (2%)
    pallas_call x1, Pallas kernels, per_device(): pl.pallas_call(functools.partial(kernel, n, nf, scale), out_shape=(jax.Sh...  30.5 us
    unnamed x4, local copies, waits for them, and re-layouts  2.93 us

profile of v6, /device:TPU:0, one launch (start us, length us, event | category | flops | bytes accessed | tf_op | source)
XLA Modules:
  0.0 34.1 jit_solution(12578616604404238500)
XLA Ops:
  0.6 30.5 %shard_map.95 = (f32[8,4,2,4096]{3,2,1,0:T(2,128)}, bf16[8,2,1024]{2,1,0:T(2,128)(2,1)}) custom-call(s32[8]{0:T(128)} %v_raw.1, s32[8]{0:T(128)} %u_raw.1, s32[8]{0:T(128)} %block_raw.1, s32[8]{0:T(128)} %count_raw.1, f32[128]{0:T(128)} %gain_re_raw.1, f32[128]{0:T(128)} %gain_im_raw.1, bf16[8,2,1024]{2,1,0:T(2,128)(2,1)} %seen_raw.1, ...), custom_call_target="tpu_custom_call" | custom-call | tf_op jit(solution)/shard_map/pallas_call | solution.py:406
  31.2 0.0 copy-start
  31.2 2.3 %copy.12 = f32[8,4,2,4096]{3,2,1,0:T(2,128)} copy(f32[8,4,2,4096]{3,2,1,0:T(2,128)} %get-tuple-element.4) | data formatting | bytes 2097152
  33.5 0.0 copy-done
  33.5 0.6 %copy.13 = bf16[8,2,1024]{2,1,0:T(2,128)(2,1)} copy(bf16[8,2,1024]{2,1,0:T(2,128)(2,1)S(1)} %copy-done) | data formatting | bytes 65536
Async XLA Ops:
  31.2 2.3 %copy-start = (bf16[8,2,1024]{2,1,0:T(2,128)(2,1)S(1)}, bf16[8,2,1024]{2,1,0:T(2,128)(2,1)}, u32[]{:S(2)}) copy-start(bf16[8,2,1024]{2,1,0:T(2,128)(2,1)} %get-tuple-element.5) | copy-start | bytes 98308

commit v7 on v6

--- a/solution.py
+++ b/solution.py
@@ -17,6 +17,7 @@
 MESH = pl.DeviceIdType.MESH
 
 LOW = 512
+SIDE = LOW // 2
 HIGH = FS // LOW
 COLS = 4
 ROWS = 8
@@ -26,9 +27,9 @@
 STEP = 16
 
 
-def cos_turns(turns):
-    away = jnp.abs(((turns + NPIX // 2) & (NPIX - 1)) - NPIX // 2)
-    x = (QUARTER - away).astype(jnp.float32) * (2.0 * math.pi / NPIX)
+def cos_turns(turns, period=NPIX):
+    away = jnp.abs(((turns + period // 2) & (period - 1)) - period // 2)
+    x = (period // 4 - away).astype(jnp.float32) * (2.0 * math.pi / period)
     x2 = x * x
     tail = -1.0 / 39916800
     for term in (362880, -5040, 120, -6):
@@ -56,17 +57,17 @@
     shape = (64, LANES)
     group = iota(shape, 0) // 8
     line = iota(shape, 0) % 8
-    facet = (line // 2 + 2) * FS
-    shift = jnp.where(line == 0, 8, 64 << line)
-    distance = jnp.where(group < 2, line, jnp.where(group < 4, line * STEP, facet))
+    facet = (line // 2 + 2) * 2 * FS + LOW - 1
+    shift = jnp.where(line == 0, STEP, jnp.where(line == 1, STEP * STEP, LOW // 2 << line))
+    distance = jnp.where(group < 2, 2 * line + 1, jnp.where(group < 4, line * 2 * STEP, facet))
     distance = jnp.where(group < 6, distance, shift)
     sine = (group == 1) | (group == 3) | (group == 7)
     quarter = jnp.where(group == 4, -(line % 2), jnp.where(group == 5, 1 - line % 2, 0))
-    return distance, jnp.where(sine, -1, quarter) * QUARTER
+    return distance, jnp.where(sine, -1, quarter) * 2 * QUARTER
 
 
 def fill_tables(f, distance, quarter, low, one, two):
-    table = cos_turns(jnp.concatenate([f] * 8, 0) * distance[...] + quarter[...])
+    table = cos_turns(jnp.concatenate([f] * 8, 0) * distance[...] + quarter[...], 2 * NPIX)
 
     def by(i):
         return table[48 + i : 49 + i], table[56 + i : 57 + i]
@@ -79,14 +80,13 @@
     fine = tuple(jnp.concatenate([x, y], 0) for x, y in zip(fine, more))
     steps = [(table[16:24], table[24:32])]
     steps.append(add(steps[0], by(1)))
-    steps += [add(step, by(2)) for step in steps[:2]]
     lines = [(table[32:40], table[40:48])]
     for i in range(3):
-        lines += [turned(*line, *by(3 + i)) for line in lines]
+        lines += [turned(*line, *by(2 + i)) for line in lines]
     for h in range(HIGH):
         one[h] = lines[h][0]
         two[h] = lines[h][1]
-    for i in range(LOW // STEP):
+    for i in range(SIDE // STEP):
         step = tuple(x[i % 8 : i % 8 + 1] for x in steps[i // 8])
         cos, sin = add(fine, step)
         rows = pl.ds(i * STEP, STEP)
@@ -99,7 +99,7 @@
     v_raw, u_raw, block_raw, count_raw, gain_re_raw, gain_im_raw, seen_raw, facet_raw,
     out_ref, res_ref,
     v_ref, u_ref, block_ref, count_ref, gain_re_ref, gain_im_ref, seen_ref, facet_four,
-    facet_ref, freq, distance, quarter, low, one, two, row_table,
+    facet_ref, plus, minus, freq, distance, quarter, low, one, two, row_table,
     seen_cells, product, strip_out, strip, model, blocks, lift, lifted, spread, image,
     v_send, v_recv, s_send, s_recv, m_send, m_recv, l_send, l_recv, in_sem,
 ):
@@ -138,6 +138,15 @@
         for t in (r, r + 1):
             both += [facet_four[t, b].astype(jnp.float32) for b in range(COLS)]
         facet_ref[pl.ds(r * 8, 16), :] = jnp.concatenate(both, 0).astype(jnp.bfloat16)
+    flip = (iota((SIDE, SIDE), 0) + iota((SIDE, SIDE), 1) == SIDE - 1).astype(jnp.float32)
+    left = [facet_ref[:, h * LOW : h * LOW + SIDE] for h in range(HIGH)]
+    right = [facet_ref[:, h * LOW + SIDE : (h + 1) * LOW] for h in range(HIGH)]
+    left = jnp.dot(
+        jnp.concatenate(left, 0), flip.astype(jnp.bfloat16), preferred_element_type=jnp.float32
+    )
+    right = jnp.concatenate(right, 0).astype(jnp.float32)
+    plus[...] = (right + left).astype(jnp.bfloat16)
+    minus[...] = (right - left).astype(jnp.bfloat16)
 
     pl.semaphore_wait(barrier, n - 1 + nf - 1)
 
@@ -222,8 +231,12 @@
         part = slice(half * HALF, (half + 1) * HALF)
         f = jnp.concatenate([freq[g][:, part], freq[g_next][:, part]], 1)
         fill_tables(f, distance, quarter, low.at[at], one.at[at], two.at[at])
-        tall = jnp.concatenate([facet_ref[:, h * LOW : (h + 1) * LOW] for h in range(HIGH)], 0)
-        product[...] = jnp.dot(tall, low[at], preferred_element_type=jnp.float32)
+        product[:, :LANES] = jnp.dot(
+            plus[...], low[at, :, :LANES], preferred_element_type=jnp.float32
+        )
+        product[:, LANES:] = jnp.dot(
+            minus[...], low[at, :, LANES:], preferred_element_type=jnp.float32
+        )
         lines_re = []
         lines_im = []
         for r in range(ROWS):
@@ -335,11 +348,14 @@
                 rows = pl.ds((h * ROWS + r) * 8, 16)
                 spread[rows, 0:LANES] = jnp.concatenate(by_cos, 0).astype(jnp.bfloat16)
                 spread[rows, LANES : 2 * LANES] = jnp.concatenate(by_sin, 0).astype(jnp.bfloat16)
-        term = lax.dot_general(
-            spread[...], low[at], (((1,), (1,)), ((), ())), preferred_element_type=jnp.float32
-        )
-        for h in range(HIGH):
-            image[:, pl.ds(h * LOW, LOW)] += term[h * 8 * ROWS : (h + 1) * 8 * ROWS]
+        for p in range(2):
+            lanes = slice(p * LANES, (p + 1) * LANES)
+            image[p] += lax.dot_general(
+                spread[:, lanes],
+                low[at, :, lanes],
+                (((1,), (1,)), ((), ())),
+                preferred_element_type=jnp.float32,
+            )
 
     def loop(first, last, step, half):
         def body(i, _):
@@ -374,10 +390,20 @@
         res_ref[s] = jnp.concatenate(lines, 0).astype(jnp.bfloat16)
 
     loop(0, pairs, grid, 1)
-    for r in range(ROWS):
-        for b in range(COLS):
-            line = r * 8 + b * 2
-            out_ref[r, b] = image[line : line + 2, :]
+    right = image[0] + image[1]
+    left = jnp.dot(
+        image[0] - image[1],
+        flip,
+        preferred_element_type=jnp.float32,
+        precision=lax.Precision.HIGHEST,
+    )
+    for h in range(HIGH):
+        rows = slice(h * 8 * ROWS, (h + 1) * 8 * ROWS)
+        both = jnp.concatenate([left[rows], right[rows]], 1)
+        for r in range(ROWS):
+            for b in range(COLS):
+                line = r * 8 + b * 2
+                out_ref[r, b, :, h * LOW : (h + 1) * LOW] = both[line : line + 2]
 
     def drain(k, _):
         v_copy(k, me).wait_send()
@@ -421,10 +447,12 @@
             pltpu.VMEM(observed.shape, bf16),
             pltpu.VMEM(facets.shape, bf16),
             pltpu.VMEM((ROWS * COLS * 2, FS), bf16),
+            pltpu.VMEM((HIGH * ROWS * 8, SIDE), bf16),
+            pltpu.VMEM((HIGH * ROWS * 8, SIDE), bf16),
             pltpu.VMEM((n, 8, LANES), jnp.int32),
             pltpu.VMEM((64, LANES), jnp.int32),
             pltpu.VMEM((64, LANES), jnp.int32),
-            pltpu.VMEM((n, LOW, 2 * LANES), bf16),
+            pltpu.VMEM((n, SIDE, 2 * LANES), bf16),
             pltpu.VMEM((n, HIGH, 8, LANES), f32),
             pltpu.VMEM((n, HIGH, 8, LANES), f32),
             pltpu.VMEM((SLOTS * 2 * SG, n * 2 * ROWS), bf16),
@@ -437,7 +465,7 @@
             pltpu.VMEM((2, n, 2 * ROWS, HALF), bf16),
             pltpu.VMEM((2, n, 2 * ROWS, HALF), bf16),
             pltpu.VMEM((HIGH * ROWS * 8, 2 * LANES), bf16),
-            pltpu.VMEM((ROWS * COLS * 2, FS), f32),
+            pltpu.VMEM((2, HIGH * ROWS * 8, SIDE), f32),
             dma((n,)), dma((n,)), dma((2, n)), dma((2, n)), dma((2, nf)), dma((2, nf)),
             dma((2, n)), dma((2, n)), dma((8,)),
         ],

time: 34.3 us -> 34.2 us (level)
  no operation moved by 1% of the time
where the time goes in v7:
time: 34.2 us; the launch traced here: 34 us
  Pallas kernels  30.4 us (89%)
  local copies, waits for them, and re-layouts  2.93 us (9%)
  between operations  0.65 us (2%)
    pallas_call x1, Pallas kernels, per_device(): pl.pallas_call(functools.partial(kernel, n, nf, scale), out_shape=(jax.Sh...  30.4 us
    unnamed x4, local copies, waits for them, and re-layouts  2.93 us

profile of v7, /device:TPU:0, one launch (start us, length us, event | category | flops | bytes accessed | tf_op | source)
XLA Modules:
  0.0 34.0 jit_solution(5834149532718880757)
XLA Ops:
  0.6 30.4 %shard_map.95 = (f32[8,4,2,4096]{3,2,1,0:T(2,128)}, bf16[8,2,1024]{2,1,0:T(2,128)(2,1)}) custom-call(s32[8]{0:T(128)} %v_raw.1, s32[8]{0:T(128)} %u_raw.1, s32[8]{0:T(128)} %block_raw.1, s32[8]{0:T(128)} %count_raw.1, f32[128]{0:T(128)} %gain_re_raw.1, f32[128]{0:T(128)} %gain_im_raw.1, bf16[8,2,1024]{2,1,0:T(2,128)(2,1)} %seen_raw.1, ...), custom_call_target="tpu_custom_call" | custom-call | tf_op jit(solution)/shard_map/pallas_call | solution.py:432
  31.1 0.0 copy-start
  31.1 2.3 %copy.12 = f32[8,4,2,4096]{3,2,1,0:T(2,128)} copy(f32[8,4,2,4096]{3,2,1,0:T(2,128)} %get-tuple-element.4) | data formatting | bytes 2097152
  33.4 0.0 copy-done
  33.4 0.6 %copy.13 = bf16[8,2,1024]{2,1,0:T(2,128)(2,1)} copy(bf16[8,2,1024]{2,1,0:T(2,128)(2,1)S(1)} %copy-done) | data formatting | bytes 65536
Async XLA Ops:
  31.1 2.3 %copy-start = (bf16[8,2,1024]{2,1,0:T(2,128)(2,1)S(1)}, bf16[8,2,1024]{2,1,0:T(2,128)(2,1)}, u32[]{:S(2)}) copy-start(bf16[8,2,1024]{2,1,0:T(2,128)(2,1)} %get-tuple-element.5) | copy-start | bytes 98308

commit v8 on v7

--- a/solution.py
+++ b/solution.py
@@ -96,12 +96,11 @@
 
 def kernel(
     n, nf, scale,
-    v_raw, u_raw, block_raw, count_raw, gain_re_raw, gain_im_raw, seen_raw, facet_raw,
+    v_ref, u_ref, block_ref, count_ref, gain_re_ref, gain_im_ref, seen_cells, facet_ref,
     out_ref, res_ref,
-    v_ref, u_ref, block_ref, count_ref, gain_re_ref, gain_im_ref, seen_ref, facet_four,
-    facet_ref, plus, minus, freq, distance, quarter, low, one, two, row_table,
-    seen_cells, product, strip_out, strip, model, blocks, lift, lifted, spread, image,
-    v_send, v_recv, s_send, s_recv, m_send, m_recv, l_send, l_recv, in_sem,
+    plus, minus, freq, distance, quarter, low, one, two, row_table,
+    product, strip_out, strip, model, blocks, lift, lifted, spread, image,
+    v_send, v_recv, s_send, s_recv, m_send, m_recv, l_send, l_recv,
 ):
     me = lax.axis_index("base")
     mf = lax.axis_index("facet")
@@ -110,14 +109,6 @@
     def device(k, j):
         return {"base": lax.rem(me + k, n), "facet": lax.rem(mf + j, nf)}
 
-    raw = [v_raw, facet_raw, seen_raw, u_raw, block_raw, count_raw, gain_re_raw, gain_im_raw]
-    held = [v_ref, facet_four, seen_ref, u_ref, block_ref, count_ref, gain_re_ref, gain_im_ref]
-    loads = [
-        pltpu.make_async_copy(src, dst, in_sem.at[i]) for i, (src, dst) in enumerate(zip(raw, held))
-    ]
-    for load in loads:
-        load.start()
-
     barrier = pltpu.get_barrier_semaphore()
 
     def greet(k, _):
@@ -128,16 +119,9 @@
     for j in range(1, nf):
         pl.semaphore_signal(barrier, inc=1, device_id=device(0, j), device_id_type=MESH)
 
-    loads[0].wait()
     freq[me] = per_lane([v_ref[s] for s in range(SLOTS)], (8, LANES)) + iota((8, LANES), 1) % SG
     distance[...], quarter[...] = phase_plan()
 
-    loads[1].wait()
-    for r in range(0, ROWS, 2):
-        both = []
-        for t in (r, r + 1):
-            both += [facet_four[t, b].astype(jnp.float32) for b in range(COLS)]
-        facet_ref[pl.ds(r * 8, 16), :] = jnp.concatenate(both, 0).astype(jnp.bfloat16)
     flip = (iota((SIDE, SIDE), 0) + iota((SIDE, SIDE), 1) == SIDE - 1).astype(jnp.float32)
     left = [facet_ref[:, h * LOW : h * LOW + SIDE] for h in range(HIGH)]
     right = [facet_ref[:, h * LOW + SIDE : (h + 1) * LOW] for h in range(HIGH)]
@@ -162,9 +146,6 @@
 
     lax.fori_loop(1, n, send_v, 0)
 
-    for load in loads[2:]:
-        load.wait()
-
     wide = n * 2 * ROWS
     lane = iota((2 * SG, wide), 1)
     sub = iota((2 * SG, wide), 0)
@@ -180,21 +161,6 @@
         return 0
 
     lax.fori_loop(0, SLOTS, fill_rows, 0)
-
-    group = iota((2 * SG, LANES), 1) // SG
-    cells = SG * SG
-    same = iota((SG, cells), 1) // SG == iota((SG, cells), 0)
-    tall = []
-    for s in range(SLOTS):
-        seen = seen_ref[s].astype(jnp.float32)
-        tall += [jnp.where(same, seen[i : i + 1], 0.0).astype(jnp.bfloat16) for i in range(2)]
-    tall = jnp.concatenate(tall, 0)
-    pick = (iota((cells, LANES), 0) % SG == iota((cells, LANES), 1) % SG).astype(jnp.float32)
-    picked = jnp.dot(tall, pick.astype(jnp.bfloat16), preferred_element_type=jnp.float32)
-    placed = jnp.zeros((2 * SG, LANES), jnp.float32)
-    for s in range(SLOTS):
-        placed = jnp.where(group == s, picked[s * 2 * SG : (s + 1) * 2 * SG], placed)
-    seen_cells[...] = placed
 
     def strip_copy(half, k, slot):
         return pltpu.make_async_remote_copy(
@@ -292,7 +258,7 @@
         gain_im = per_lane([gain_im_ref[block_ref[s]] for s in range(SLOTS)], full)[:, part]
         weight = per_lane([count_ref[s] for s in range(SLOTS)], full)[:, part]
         weight = weight.astype(jnp.float32) / CMAX
-        seen = seen_cells[:, part]
+        seen = seen_cells[:, part].astype(jnp.float32)
         for j in range(1, nf):
             model_copy(half, j, lax.rem(mf + nf - j, nf)).wait_recv()
         whole = model[half, 0].astype(jnp.float32)
@@ -305,6 +271,7 @@
         res_re = weight * (gain_re * diff_re + gain_im * diff_im)
         res_im = weight * (gain_re * diff_im - gain_im * diff_re)
         residual = jnp.concatenate([res_re, res_im], 0)
+        res_ref[:, part] = residual.astype(jnp.bfloat16)
         blocks[half] = jnp.concatenate(
             [
                 jnp.where(owner == s, residual, 0.0).astype(jnp.bfloat16)
@@ -376,19 +343,6 @@
     raise_rows(1)
     loop(middle, pairs, grid, 0)
 
-    grow = (iota((HALF, cells), 0) % SG == iota((HALF, cells), 1) % SG).astype(jnp.float32)
-    grown = jnp.dot(
-        blocks[...].reshape(2 * half_rows, HALF),
-        grow.astype(jnp.bfloat16),
-        preferred_element_type=jnp.float32,
-    )
-    for s in range(SLOTS):
-        lines = [
-            jnp.sum(jnp.where(same, grown[i * SG : (i + 1) * SG], 0.0), 0, keepdims=True)
-            for i in (2 * s, 2 * s + 1)
-        ]
-        res_ref[s] = jnp.concatenate(lines, 0).astype(jnp.bfloat16)
-
     loop(0, pairs, grid, 1)
     right = image[0] + image[1]
     left = jnp.dot(
@@ -400,10 +354,7 @@
     for h in range(HIGH):
         rows = slice(h * 8 * ROWS, (h + 1) * 8 * ROWS)
         both = jnp.concatenate([left[rows], right[rows]], 1)
-        for r in range(ROWS):
-            for b in range(COLS):
-                line = r * 8 + b * 2
-                out_ref[r, b, :, h * LOW : (h + 1) * LOW] = both[line : line + 2]
+        out_ref[:, h * LOW : (h + 1) * LOW] = both
 
     def drain(k, _):
         v_copy(k, me).wait_send()
@@ -424,29 +375,22 @@
     assert facets.shape == (ROWS, COLS, 2, FS) and nf * COLS == NF and n % 2 == 0
     assert observed.shape == (SLOTS, 2, SG * SG)
     scale = 1.0 / math.sqrt(NF * n * ROWS * FS)
-    hbm = pl.BlockSpec(memory_space=pltpu.HBM)
+    rows = facets.reshape(ROWS * COLS * 2, FS)
+    seen = observed.reshape(SLOTS, 2, SG, SG).transpose(1, 2, 0, 3).reshape(2 * SG, LANES)
+    smem = pl.BlockSpec(memory_space=pltpu.SMEM)
     vmem = pl.BlockSpec(memory_space=pltpu.VMEM)
     bf16 = jnp.bfloat16
     f32 = jnp.float32
     dma = pltpu.SemaphoreType.DMA
-    return pl.pallas_call(
+    out, res = pl.pallas_call(
         functools.partial(kernel, n, nf, scale),
         out_shape=(
-            jax.ShapeDtypeStruct(facets.shape, f32),
-            jax.ShapeDtypeStruct(observed.shape, bf16),
+            jax.ShapeDtypeStruct((ROWS * COLS * 2, FS), f32),
+            jax.ShapeDtypeStruct((2 * SG, LANES), bf16),
         ),
-        in_specs=[hbm] * 8,
+        in_specs=[smem] * 6 + [vmem] * 2,
         out_specs=(vmem, vmem),
         scratch_shapes=[
-            pltpu.SMEM((SLOTS,), jnp.int32),
-            pltpu.SMEM((SLOTS,), jnp.int32),
-            pltpu.SMEM((SLOTS,), jnp.int32),
-            pltpu.SMEM((SLOTS,), jnp.int32),
-            pltpu.SMEM(gain_real.shape, f32),
-            pltpu.SMEM(gain_imag.shape, f32),
-            pltpu.VMEM(observed.shape, bf16),
-            pltpu.VMEM(facets.shape, bf16),
-            pltpu.VMEM((ROWS * COLS * 2, FS), bf16),
             pltpu.VMEM((HIGH * ROWS * 8, SIDE), bf16),
             pltpu.VMEM((HIGH * ROWS * 8, SIDE), bf16),
             pltpu.VMEM((n, 8, LANES), jnp.int32),
@@ -456,7 +400,6 @@
             pltpu.VMEM((n, HIGH, 8, LANES), f32),
             pltpu.VMEM((n, HIGH, 8, LANES), f32),
             pltpu.VMEM((SLOTS * 2 * SG, n * 2 * ROWS), bf16),
-            pltpu.VMEM((2 * SG, LANES), f32),
             pltpu.VMEM((HIGH * ROWS * 8, 2 * LANES), f32),
             pltpu.VMEM((2, n, 2 * ROWS, HALF), bf16),
             pltpu.VMEM((2, n, 2 * ROWS, HALF), bf16),
@@ -467,12 +410,14 @@
             pltpu.VMEM((HIGH * ROWS * 8, 2 * LANES), bf16),
             pltpu.VMEM((2, HIGH * ROWS * 8, SIDE), f32),
             dma((n,)), dma((n,)), dma((2, n)), dma((2, n)), dma((2, nf)), dma((2, nf)),
-            dma((2, n)), dma((2, n)), dma((8,)),
+            dma((2, n)), dma((2, n)),
         ],
         compiler_params=pltpu.CompilerParams(
-            collective_id=0, has_side_effects=True, vmem_limit_bytes=62 * 1024 * 1024
+            collective_id=0, has_side_effects=True, vmem_limit_bytes=48 * 1024 * 1024
         ),
-    )(sub_v, sub_u, sub_block, sub_count, gain_real, gain_imag, observed, facets)
+    )(sub_v, sub_u, sub_block, sub_count, gain_real, gain_imag, seen, rows)
+    res = res.reshape(2, SG, SLOTS, SG).transpose(2, 0, 1, 3)
+    return (out.reshape(ROWS, COLS, 2, FS), res.reshape(SLOTS, 2, SG * SG))
 
 
 def solution(mesh):

time: 34.2 us -> 35.1 us (1.026)
  local copies, waits for them, and re-layouts: 2.93 us -> 4.37 us
  Pallas kernels: 30.4 us -> 29.8 us
    reshape x0 -> x7, local copies, waits for them, and re-layouts: none -> 3.87 us  [the longest x2 2.37 us: per_device(): return (out.reshape(ROWS, COLS, 2, FS), res.reshape(SLOTS, 2, SG * SG))]
    unnamed x4 -> x14, local copies, waits for them, and re-layouts: 2.93 us -> 0.49 us
    pallas_call x1, Pallas kernels: 30.4 us -> 29.8 us  [per_device(): pl.pallas_call(functools.partial(kernel, n, nf, scale), out_shape=(jax.Sh...]
where the time goes in v8:
time: 35.1 us; the launch traced here: 35 us
  Pallas kernels  29.8 us (85%)
  local copies, waits for them, and re-layouts  4.37 us (12%)
  between operations  0.74 us (2%)
    pallas_call x1, Pallas kernels, per_device(): pl.pallas_call(functools.partial(kernel, n, nf, scale), out_shape=(jax.Sh...  29.8 us
    reshape x2, local copies, waits for them, and re-layouts, per_device(): return (out.reshape(ROWS, COLS, 2, FS), res.reshape(SLOTS, 2, SG * SG))  2.37 us
    reshape x3, local copies, waits for them, and re-layouts, per_device(): observed.reshape(SLOTS, 2, SG, SG).transpose(1, 2, 0, 3)  1.17 us

profile of v8, /device:TPU:0, one launch (start us, length us, event | category | flops | bytes accessed | tf_op | source)
XLA Modules:
  0.0 35.0 jit_solution(1947545573859256430)
XLA Ops:
  0.6 0.0 copy-start.6
  0.6 1.0 %reshape.22 = bf16[8,2,32,32]{3,2,1,0:T(8,128)(2,1)S(1)} reshape(bf16[8,2,1024]{2,1,0:T(2,128)(2,1)} %param.9) | data formatting | bytes 65536 | tf_op jit(solution)/shard_map/reshape | solution.py:379
  1.6 0.1 copy.13
  1.7 0.1 reshape.23.seen_cells
  1.8 0.0 copy-done.6
  1.8 0.0 copy-start
  1.8 0.0 copy-start.1
  1.9 0.0 copy-start.2
  1.9 0.0 copy-start.3
  1.9 0.0 copy-start.4
  1.9 0.0 copy-start.5
  1.9 0.2 reshape.24.facet_ref
  2.1 0.4 %copy-done = s32[8]{0:T(128)S(1)} copy-done((s32[8]{0:T(128)S(1)}, s32[8]{0:T(128)}, u32[]{:S(2)}) %copy-start) | copy-done | bytes 56
  2.5 0.0 copy-done.1
  2.5 0.0 copy-done.2
  2.5 0.0 copy-done.3
  2.5 0.0 copy-done.4
  2.6 0.0 copy-done.5
  2.6 29.8 %shard_map.95 = (f32[64,4096]{1,0:T(8,128)S(1)}, bf16[64,256]{1,0:T(8,128)(2,1)S(1)}) custom-call(s32[8]{0:T(128)S(1)} %copy-done, s32[8]{0:T(128)S(1)} %copy-done.1, s32[8]{0:T(128)S(1)} %copy-done.2, s32[8]{0:T(128)S(1)} %copy-done.3, f32[128]{0:T(128)S(1)} %copy-done.4, f32[128]{0:T(128)S(1)} %copy-done.5, bf16[64,256]{1,0:T(8,128)(2,1)S(1)} %reshape.23.seen_cells, ...), custom_call_target="tpu_custom_call" | custom-call | tf_op jit(solution)/shard_map/pallas_call | solution.py:385
  32.4 1.6 %reshape.25 = f32[8,4,2,4096]{3,2,1,0:T(2,128)} reshape(f32[64,4096]{1,0:T(8,128)S(1)} %get-tuple-element.4) | data formatting | bytes 2097152 | tf_op jit(solution)/shard_map/reshape | solution.py:420
  34.0 0.1 reshape.26
  34.2 0.8 %reshape.27 = bf16[8,2,1024]{2,1,0:T(2,128)(2,1)} reshape(bf16[8,2,32,32]{3,2,1,0:T(8,128)(2,1)S(1)} %copy.11) | data formatting | bytes 65536 | tf_op jit(solution)/shard_map/reshape | solution.py:420
  (1 shorter events, 0.0 us)
Async XLA Ops:
  0.6 1.2 %copy-start.6 = (bf16[8,4,2,4096]{3,2,1,0:T(2,128)(2,1)S(1)}, bf16[8,4,2,4096]{3,2,1,0:T(2,128)(2,1)}, u32[]{:S(2)}) copy-start(bf16[8,4,2,4096]{3,2,1,0:T(2,128)(2,1)} %param.8) | copy-start | bytes 1572868
  1.8 0.7 %copy-start = (s32[8]{0:T(128)S(1)}, s32[8]{0:T(128)}, u32[]{:S(2)}) copy-start(s32[8]{0:T(128)} %v_ref.1) | copy-start | bytes 100
  1.8 0.7 %copy-start.1 = (s32[8]{0:T(128)S(1)}, s32[8]{0:T(128)}, u32[]{:S(2)}) copy-start(s32[8]{0:T(128)} %u_ref.1) | copy-start | bytes 100
  1.9 0.7 %copy-start.2 = (s32[8]{0:T(128)S(1)}, s32[8]{0:T(128)}, u32[]{:S(2)}) copy-start(s32[8]{0:T(128)} %block_ref.1) | copy-start | bytes 100
  1.9 0.7 %copy-start.3 = (s32[8]{0:T(128)S(1)}, s32[8]{0:T(128)}, u32[]{:S(2)}) copy-start(s32[8]{0:T(128)} %count_ref.1) | copy-start | bytes 100
  1.9 0.7 %copy-start.4 = (f32[128]{0:T(128)S(1)}, f32[128]{0:T(128)}, u32[]{:S(2)}) copy-start(f32[128]{0:T(128)} %gain_re_ref.1) | copy-start | bytes 1540
  1.9 0.7 %copy-start.5 = (f32[128]{0:T(128)S(1)}, f32[128]{0:T(128)}, u32[]{:S(2)}) copy-start(f32[128]{0:T(128)} %gain_im_ref.1) | copy-start | bytes 1540
